TPU v7x, 512 devices: a whole 4x4x16 slice. The times are simulated.
512 devices in a mesh: slab: 16 (over z), head: 8 (over y, core), seq: 4 (over x).
Axes of the slice: x: 4, y: 4, z: 16, core: 2. Of those that a mesh axis runs over, the one named last changes fastest.
Arguments:
- qkv: bfloat16 [3, 64, 384, 4096], P(None, ('slab', 'seq'), 'head'), may hold values from -6 to 6
- pattern: int32 [64, 5], P('slab'), may hold values from 0 to 1, as said below
- counts: int32 [16], replicated, may hold values from 1 to 4, as said below
Outputs:
- attended: bfloat16 [64, 384, 4096], P(('slab', 'seq'), 'head')
Inputs may be any that keep to these rules, and one draw needn't show every extreme that they name: Slab s holds counts[s] live tiles, in slots 0 to counts[s] - 1 of its 4; in every draw one slab holds 4 and one holds 1. `pattern`: the first tile of every slab has 1 in columns 3 and 4.
All inputs are finite; a program needn't handle non-finite values.
Results may differ from a plain program's by a relative error of at most 0.0049.
Values may be sent and summed in bfloat16 or wider, within the bound.
No kernel may reach another device: no remote copies, remote signals or barrier semaphores. Data moves between devices by JAX's collectives and lax.ppermute only.
A program may use at most 64 MiB of HBM per device.

v0:
```python
import math

import jax
import jax.numpy as jnp
import numpy as np
from jax import lax
from jax.sharding import PartitionSpec as P

HEAD_DIM = 128


def passed_along(value, axis, by):
    length = lax.axis_size(axis)
    pairs = [(i, i + by) for i in range(length) if 0 <= i + by < length]
    return lax.ppermute(value, axis, pairs)


def pick_count(counts, slab_rows):
    slab_ids = jnp.arange(counts.shape[0], dtype=jnp.int32)
    return jnp.sum(jnp.where(slab_rows[..., None] == slab_ids, counts, 0), axis=-1)


def tile_plan(pattern_rows, counts, slab_rows, group_ids, places, group_total, per_group):
    slab_total = counts.shape[0]
    first_slot = group_ids * per_group
    always = jnp.ones(first_slot.shape, dtype=bool)
    slot_list = [first_slot + 0]
    slot_list = slot_list + [
        first_slot - 1,
        first_slot + per_group,
        first_slot + per_group - 1,
        first_slot,
    ]
    slab_list = [slab_rows] * (per_group + 2) + [slab_rows - 1, slab_rows + 1]
    exist_list = [always] * per_group + [
        group_ids >= 1,
        group_ids + 1 < group_total,
        slab_rows >= 1,
        slab_rows + 1 < slab_total,
    ]
    key_slot = jnp.stack(slot_list, axis=1)
    key_slab = jnp.stack(slab_list, axis=1)
    exists = jnp.stack(exist_list, axis=1)
    live_key = exists & (key_slot < pick_count(counts, key_slab))
    columns = jnp.arange(per_group + 4, dtype=jnp.int32)
    allowed = ((pattern_rows == 1) | (columns[None, :] == places[:, None])) & live_key
    live_query = first_slot + places < pick_count(counts, slab_rows)
    return (allowed, live_query, key_slab, key_slot)


def attend(query_rows, key_rows, value_rows, allowed, live_query):
    per_group, cand_count = allowed.shape
    tile_len = query_rows.shape[0] // per_group
    score_scale = 1.0 / math.sqrt(query_rows.shape[-1])
    scores = (
        jnp.einsum("qd,kd->qk", query_rows, key_rows, preferred_element_type=jnp.float32)
        * score_scale
    )
    scores = scores.reshape(per_group, tile_len, cand_count, tile_len)
    usable = allowed[:, None, :, None]
    peak_score = jnp.max(jnp.where(usable, scores, -1e30), axis=(2, 3), keepdims=True)
    weights = jnp.where(usable, jnp.exp(scores - peak_score), 0.0)
    totals = jnp.sum(weights, axis=(2, 3), keepdims=True)
    totals = jnp.where(live_query[:, None, None, None], totals, 1.0)
    shares = (
        (weights / totals).astype(jnp.bfloat16).reshape(per_group * tile_len, cand_count * tile_len)
    )
    mixed_out = jnp.dot(shares, value_rows, preferred_element_type=jnp.float32)
    mixed_out = mixed_out.reshape(per_group, tile_len, -1)
    mixed_out = jnp.where(live_query[:, None, None], mixed_out, 0.0)
    return mixed_out.astype(jnp.bfloat16).reshape(per_group * tile_len, -1)


def on_device(qkv, pattern, counts):
    seq_count = lax.axis_size("seq")
    slab_index = lax.axis_index("slab")
    per_group = qkv.shape[1]
    relaid = lax.all_to_all(
        lax.all_to_all(qkv, "head", split_axis=3, concat_axis=2, tiled=True),
        "seq",
        split_axis=3,
        concat_axis=1,
        tiled=True,
    )
    group_ids = jnp.arange(seq_count * per_group, dtype=jnp.int32) // per_group
    row_count = relaid.shape[1]
    group_local = row_count // per_group
    tile_len = relaid.shape[2]
    width = relaid.shape[3]
    head_local = width // HEAD_DIM
    cand_count = per_group + 4
    key_tiles = relaid[1:3]
    from_below = passed_along(key_tiles, "slab", 1)
    from_above = passed_along(key_tiles, "slab", -1)
    blank_tile = jnp.zeros_like(key_tiles[:, :1])
    padded = jnp.concatenate([blank_tile, key_tiles, blank_tile], axis=1)
    bank_source = jnp.concatenate([padded, from_below, from_above], axis=1)
    padded_len = row_count + 2
    table = np.array(
        [
            [group_pos * per_group + 1]
            + [
                group_pos * per_group,
                (group_pos + 1) * per_group + 1,
                padded_len + group_pos,
                padded_len + group_local + group_pos,
            ]
            for group_pos in range(group_local)
        ],
        dtype=np.int32,
    )
    key_banks = jnp.take(bank_source, jnp.asarray(table), axis=1)
    key_banks = key_banks.reshape(2, group_local, cand_count, tile_len, head_local, HEAD_DIM)
    key_banks = key_banks.transpose(1, 4, 0, 2, 3, 5).reshape(
        group_local * head_local, 2, cand_count * tile_len, HEAD_DIM
    )
    item_queries = relaid[0].reshape(group_local, per_group * tile_len, head_local, HEAD_DIM)
    item_queries = item_queries.transpose(0, 2, 1, 3).reshape(
        group_local * head_local, per_group * tile_len, HEAD_DIM
    )
    places = jnp.arange(row_count, dtype=jnp.int32) % per_group
    slab_rows = jnp.zeros((row_count,), jnp.int32) + slab_index
    allowed, live_query, key_slab, key_slot = tile_plan(
        pattern, counts, slab_rows, group_ids, places, seq_count, per_group
    )
    item_allowed = jnp.repeat(
        allowed.reshape(group_local, per_group, cand_count), head_local, axis=0
    )
    item_live = jnp.repeat(live_query.reshape(group_local, per_group), head_local, axis=0)

    def attend_item(packed):
        return attend(packed[0], packed[1][0], packed[1][1], packed[2], packed[3])

    attended = lax.map(attend_item, (item_queries, key_banks, item_allowed, item_live))
    attended = attended.reshape(group_local, head_local, per_group, tile_len, HEAD_DIM)
    attended = attended.transpose(0, 2, 3, 1, 4).reshape(row_count, tile_len, width)
    shaped = attended.reshape(row_count, tile_len, 1, 1, width)
    returned = lax.all_to_all(
        lax.all_to_all(shaped, "head", split_axis=1, concat_axis=2, tiled=True),
        "seq",
        split_axis=0,
        concat_axis=3,
        tiled=True,
    )
    return returned.reshape(returned.shape[0], returned.shape[1], -1)


def solution(mesh):
    in_specs = (P(None, ("slab", "seq"), "head", None), P("slab", None), P())
    out_specs = P(("slab", "seq"), "head", None)
    return jax.shard_map(
        on_device, mesh=mesh, in_specs=in_specs, out_specs=out_specs, check_vma=False
    )
```

profile of v0, /device:TPU:1, one launch (start us, length us, event | category | flops | bytes accessed | tf_op | source)
XLA Modules:
  0.0 162.9 jit_solution(17467221125982786893)
XLA Ops:
  0.0 6.2 %copy.59 = bf16[3,1,48,4096]{2,0,1,3:T(4,128)(2,1)} copy(bf16[3,1,48,4096]{3,2,1,0:T(8,128)(2,1)} %param.6) | data formatting | bytes 2359296 | tf_op args[0]
  6.2 0.0 copy-start
  6.2 8.1 %reshape.125 = bf16[8,2,36864]{2,1,0:T(2,128)(2,1)} reshape(bf16[4096,1,3,48]{3,2,1,0:T(4,128)(2,1)} %bitcast.78) | data formatting | bytes 2359296
  14.2 10.3 %all-to-all-start = ((bf16[8,2,36864]{2,1,0:T(2,128)(2,1)}), bf16[8,2,36864]{2,1,0:T(2,128)(2,1)S(1)}, u32[]{:S(2)}, u32[]{:S(2)}) async-start(bf16[8,2,36864]{2,1,0:T(2,128)(2,1)} %reshape.125), calls=%async_computation | async-start | bytes 2359296 | tf_op jit(solution)/shard_map/all_to_all | solution.py:79
  24.6 0.0 copy-done
  24.6 0.1 copy.57
  24.8 16.3 %all-to-all-done = bf16[8,2,36864]{2,1,0:T(2,128)(2,1)S(1)} async-done(((bf16[8,2,36864]{2,1,0:T(2,128)(2,1)}), bf16[8,2,36864]{2,1,0:T(2,128)(2,1)S(1)}, u32[]{:S(2)}, u32[]{:S(2)}) %all-to-all-start) | async-done | bytes 1179680 | tf_op jit(solution)/shard_map/all_to_all | solution.py:79
  41.1 6.6 %reshape.126 = bf16[4096,1,3,48]{3,2,1,0:T(4,128)(2,1)} reshape(bf16[8,2,36864]{2,1,0:T(2,128)(2,1)S(1)} %all-to-all-done) | data formatting | bytes 2359296
  47.7 5.4 %copy.74 = bf16[3,1,48,8,512]{4,2,3,0,1:T(8,128)(2,1)S(1)} copy(bf16[3,1,48,8,512]{2,0,4,3,1:T(4,128)(2,1)} %bitcast.77) | data formatting | bytes 2359296 | tf_op jit(solution)/shard_map/all_to_all | solution.py:79
  53.1 0.0 copy-start.1
  53.1 2.3 %copy.62 = bf16[3,1,384,512]{2,0,1,3:T(4,128)(2,1)} copy(bf16[3,1,384,512]{3,2,0,1:T(8,128)(2,1)S(1)} %bitcast.84) | data formatting | bytes 2359296 | tf_op jit(solution)/shard_map/all_to_all | solution.py:79
  55.4 3.6 %all-to-all-start.1 = ((bf16[3,1,384,512]{2,0,1,3:T(4,128)(2,1)}), bf16[3,1,384,512]{2,0,1,3:T(4,128)(2,1)S(1)}, u32[]{:S(2)}, u32[]{:S(2)}) async-start(bf16[3,1,384,512]{2,0,1,3:T(4,128)(2,1)} %copy.62), calls=%async_computation.1 | async-start | bytes 3145728 | tf_op jit(solution)/shard_map/all_to_all | solution.py:78
  58.9 0.0 copy-start.2
  59.1 0.0 copy-done.1
  59.1 0.1 select_reduce_fusion.2
  59.2 0.2 select_reduce_fusion.1
  59.5 19.4 %all-to-all-done.1 = bf16[3,1,384,512]{2,0,1,3:T(4,128)(2,1)S(1)} async-done(((bf16[3,1,384,512]{2,0,1,3:T(4,128)(2,1)}), bf16[3,1,384,512]{2,0,1,3:T(4,128)(2,1)S(1)}, u32[]{:S(2)}, u32[]{:S(2)}) %all-to-all-start.1) | async-done | bytes 1179680 | tf_op jit(solution)/shard_map/all_to_all | solution.py:78
  78.8 0.2 copy.63
  79.0 0.1 slice_bitcast_fusion
  79.1 2.2 %collective-permute-start = (bf16[2,4,384,128]{2,3,1,0:T(8,128)(2,1)S(1)}, bf16[2,4,384,128]{2,3,1,0:T(8,128)(2,1)}, u32[]{:S(2)}, u32[]{:S(2)}) collective-permute-start(bf16[2,4,384,128]{2,3,1,0:T(8,128)(2,1)S(1)} %slice_bitcast_fusion), channel_id=1, source_target_pairs={{0,32},{32,64},{64,96},{96,128},{128,160},{160,192},{192,224},{224... | collective-permute-start | bytes 2359304 | tf_op jit(solution)/shard_map/ppermute | solution.py:15
  81.3 0.7 broadcast_dynamic-update-slice_fusion
  81.9 1.3 collective-permute-start.1
  83.2 0.0 copy-done.2
  83.3 0.1 copy.66
  83.4 1.0 constant_dynamic-update-slice_fusion.2
  84.4 0.7 broadcast_dynamic-update-slice_fusion.1
  85.1 10.6 %collective-permute-done = bf16[2,4,384,128]{2,3,1,0:T(8,128)(2,1)} collective-permute-done((bf16[2,4,384,128]{2,3,1,0:T(8,128)(2,1)S(1)}, bf16[2,4,384,128]{2,3,1,0:T(8,128)(2,1)}, u32[]{:S(2)}, u32[]{:S(2)}) %collective-permute-start) | collective-permute-done | bytes 786464 | tf_op jit(solution)/shard_map/ppermute | solution.py:15
  95.7 2.1 %constant_dynamic-update-slice_fusion.1 = bf16[2,14,384,128]{2,3,1,0:T(8,128)(2,1)} fusion(bf16[2,14,384,128]{2,3,1,0:T(8,128)(2,1)} %broadcast_dynamic-update-slice_fusion.1, bf16[2,4,384,128]{2,3,1,0:T(8,128)(2,1)} %collective-permute-done), kind=kLoop, calls=%fused_computation.28 | loop fusion | bytes 1572864
  97.8 3.3 %collective-permute-done.1 = bf16[2,4,384,128]{2,3,1,0:T(8,128)(2,1)S(1)} collective-permute-done((bf16[2,4,384,128]{2,3,1,0:T(8,128)(2,1)S(1)}, bf16[2,4,384,128]{2,3,1,0:T(8,128)(2,1)S(1)}, u32[]{:S(2)}, u32[]{:S(2)}) %collective-permute-start.1) | collective-permute-done | bytes 786464 | tf_op jit(solution)/shard_map/ppermute | solution.py:15
  101.1 1.0 constant_dynamic-update-slice_fusion
  102.1 5.1 %gather_fusion = bf16[20,2,384,128]{2,3,1,0:T(8,128)(2,1)} fusion(bf16[2,14,384,128]{2,3,1,0:T(8,128)(2,1)} %constant_dynamic-update-slice_fusion, s32[1024]{0:T(1024)S(1)} %pad_clamp_fusion), kind=kCustom, calls=%fused_computation | custom fusion | bytes 7864400 | tf_op jit(solution)/shard_map/jit(_take)/gather | solution.py:112
  107.2 6.3 %copy.64 = bf16[4,1,2,5,384,128]{5,4,3,2,0,1:T(8,128)(2,1)} copy(bf16[4,1,2,5,384,128]{4,5,2,3,0,1:T(8,128)(2,1)} %bitcast.79) | data formatting | bytes 7864320 | tf_op jit(solution)/shard_map/transpose | solution.py:114
  113.5 24.8 %while.10 = (s32[]{:T(128)}, bf16[4,384,128]{2,1,0:T(8,128)(2,1)S(1)}, pred[4,1]{0,1:T(4,128)(4,1)S(1)}, pred[4,1,5]{2,1,0:T(4,128)(4,1)S(1)}, bf16[4,384,128]{1...) while((s32[]{:T(128)}, bf16[4,384,128]{2,1,0:T(8,128)(2,1)S(1)}, ...), condition=%wide.region_5.6_spmd, body=%wide.region_2.5_spmd.sunk | while | flops 384958080 | bytes 10053771 | solution.py:134
  113.5 0.6 constant_dynamic-slice_fusion.2
  114.1 0.1 broadcast_in_dim.162
  114.2 1.7 %select_reduce_fusion.4 = (f32[384]{0:T(512)S(1)}, f32[384,1920]{1,0:T(8,128)S(1)}) fusion(pred[1920]{0:T(1024)(128)(4,1)S(1)} %broadcast_in_dim.163, bf16[4,2,1920,128]{3,2,1,0:T(8,128)(2,1)} %get-tuple-element.162, s32[]{:T(128)S(6)} %copy.88, bf16[4,384,128]{1,2,0:T(8,128)(2,1)S(1)} %get-tuple-element.161), kind=kOutput, calls=%fused_computation.4.clone.1 | convolution fusion | flops 190955136 | bytes 3543552 | tf_op jit(solution)/shard_map/while/body/eval_jaxpr/qd,kd->qk/dot_general | solution.py:56
  115.9 0.6 fusion.16
  116.5 0.6 broadcast_select_fusion.2
  117.2 2.5 %fusion.17 = bf16[4,384,128]{2,1,0:T(8,128)(2,1)S(1)} fusion(bf16[4,384,128]{2,1,0:T(8,128)(2,1)S(1)} %get-tuple-element.149, s32[]{:T(128)S(6)} %copy.88, f32[384,1920]{1,0:T(8,128)S(1)} %get-tuple-element.137, f32[384]{0:T(512)S(1)} %broadcast_select_fusion.2, f32[384]{0:T(512)S(1)} %get-tuple-element.138, ...), kind=kOutput, calls=%fused_computation.10.clone.1 | convolution fusion | flops 191791104 | bytes 3547136 | tf_op jit(solution)/shard_map/while/body/eval_jaxpr/dot_general | solution.py:68
  119.7 0.6 constant_dynamic-slice_fusion.2
  120.3 0.1 broadcast_in_dim.162
  120.4 1.7 %select_reduce_fusion.4 = (f32[384]{0:T(512)S(1)}, f32[384,1920]{1,0:T(8,128)S(1)}) fusion(pred[1920]{0:T(1024)(128)(4,1)S(1)} %broadcast_in_dim.163, bf16[4,2,1920,128]{3,2,1,0:T(8,128)(2,1)} %get-tuple-element.162, s32[]{:T(128)S(6)} %copy.88, bf16[4,384,128]{1,2,0:T(8,128)(2,1)S(1)} %get-tuple-element.161), kind=kOutput, calls=%fused_computation.4.clone.1 | convolution fusion | flops 190955136 | bytes 3543552 | tf_op jit(solution)/shard_map/while/body/eval_jaxpr/qd,kd->qk/dot_general | solution.py:56
  122.1 0.6 fusion.16
  122.7 0.6 broadcast_select_fusion.2
  123.4 2.5 %fusion.17 = bf16[4,384,128]{2,1,0:T(8,128)(2,1)S(1)} fusion(bf16[4,384,128]{2,1,0:T(8,128)(2,1)S(1)} %get-tuple-element.149, s32[]{:T(128)S(6)} %copy.88, f32[384,1920]{1,0:T(8,128)S(1)} %get-tuple-element.137, f32[384]{0:T(512)S(1)} %broadcast_select_fusion.2, f32[384]{0:T(512)S(1)} %get-tuple-element.138, ...), kind=kOutput, calls=%fused_computation.10.clone.1 | convolution fusion | flops 191791104 | bytes 3547136 | tf_op jit(solution)/shard_map/while/body/eval_jaxpr/dot_general | solution.py:68
  125.9 0.6 constant_dynamic-slice_fusion.2
  126.5 0.1 broadcast_in_dim.162
  126.6 1.7 %select_reduce_fusion.4 = (f32[384]{0:T(512)S(1)}, f32[384,1920]{1,0:T(8,128)S(1)}) fusion(pred[1920]{0:T(1024)(128)(4,1)S(1)} %broadcast_in_dim.163, bf16[4,2,1920,128]{3,2,1,0:T(8,128)(2,1)} %get-tuple-element.162, s32[]{:T(128)S(6)} %copy.88, bf16[4,384,128]{1,2,0:T(8,128)(2,1)S(1)} %get-tuple-element.161), kind=kOutput, calls=%fused_computation.4.clone.1 | convolution fusion | flops 190955136 | bytes 3543552 | tf_op jit(solution)/shard_map/while/body/eval_jaxpr/qd,kd->qk/dot_general | solution.py:56
  128.3 0.6 fusion.16
  129.0 0.6 broadcast_select_fusion.2
  129.6 2.5 %fusion.17 = bf16[4,384,128]{2,1,0:T(8,128)(2,1)S(1)} fusion(bf16[4,384,128]{2,1,0:T(8,128)(2,1)S(1)} %get-tuple-element.149, s32[]{:T(128)S(6)} %copy.88, f32[384,1920]{1,0:T(8,128)S(1)} %get-tuple-element.137, f32[384]{0:T(512)S(1)} %broadcast_select_fusion.2, f32[384]{0:T(512)S(1)} %get-tuple-element.138, ...), kind=kOutput, calls=%fused_computation.10.clone.1 | convolution fusion | flops 191791104 | bytes 3547136 | tf_op jit(solution)/shard_map/while/body/eval_jaxpr/dot_general | solution.py:68
  132.1 0.6 constant_dynamic-slice_fusion.2
  132.7 0.1 broadcast_in_dim.162
  132.8 1.7 %select_reduce_fusion.4 = (f32[384]{0:T(512)S(1)}, f32[384,1920]{1,0:T(8,128)S(1)}) fusion(pred[1920]{0:T(1024)(128)(4,1)S(1)} %broadcast_in_dim.163, bf16[4,2,1920,128]{3,2,1,0:T(8,128)(2,1)} %get-tuple-element.162, s32[]{:T(128)S(6)} %copy.88, bf16[4,384,128]{1,2,0:T(8,128)(2,1)S(1)} %get-tuple-element.161), kind=kOutput, calls=%fused_computation.4.clone.1 | convolution fusion | flops 190955136 | bytes 3543552 | tf_op jit(solution)/shard_map/while/body/eval_jaxpr/qd,kd->qk/dot_general | solution.py:56
  134.5 0.6 fusion.16
  135.2 0.6 broadcast_select_fusion.2
  135.8 2.5 %fusion.17 = bf16[4,384,128]{2,1,0:T(8,128)(2,1)S(1)} fusion(bf16[4,384,128]{2,1,0:T(8,128)(2,1)S(1)} %get-tuple-element.149, s32[]{:T(128)S(6)} %copy.88, f32[384,1920]{1,0:T(8,128)S(1)} %get-tuple-element.137, f32[384]{0:T(512)S(1)} %broadcast_select_fusion.2, f32[384]{0:T(512)S(1)} %get-tuple-element.138, ...), kind=kOutput, calls=%fused_computation.10.clone.1 | convolution fusion | flops 191791104 | bytes 3547136 | tf_op jit(solution)/shard_map/while/body/eval_jaxpr/dot_general | solution.py:68
  138.3 0.3 copy.80
  138.6 13.2 %all_to_all.66 = bf16[4,384,1,1,128]{4,0,3,2,1:T(4,128)(2,1)S(1)} all-to-all(bf16[4,384,1,1,128]{4,0,3,2,1:T(4,128)(2,1)S(1)} %bitcast.85), channel_id=1, replica_groups=mesh['slab'=16,'head'=8,'seq'=4] {'head'}, dimensions={1} | all-to-all | bytes 786432 | tf_op jit(solution)/shard_map/all_to_all | solution.py:139
  151.8 0.3 copy.79
  152.0 9.6 %all_to_all.67 = bf16[4,48,8,1,128]{4,2,1,3,0:T(8,128)(2,1)S(1)} all-to-all(bf16[4,48,8,1,128]{4,2,1,3,0:T(8,128)(2,1)S(1)} %bitcast.87), channel_id=1, replica_groups=mesh['slab'=16,'head'=8,'seq'=4] {'seq'}, dimensions={0} | all-to-all | bytes 786432 | tf_op jit(solution)/shard_map/all_to_all | solution.py:138
  161.6 0.3 copy.70
  161.9 1.0 reshape.115
  (26 shorter events, 0.3 us)
Async XLA Ops:
  6.2 18.4 %copy-start = (s32[4,5]{1,0:T(4,128)S(1)}, s32[4,5]{1,0:T(4,128)}, u32[]{:S(2)}) copy-start(s32[4,5]{1,0:T(4,128)} %param.7) | copy-start | bytes 244
  14.2 26.9 %all-to-all-start = ((bf16[8,2,36864]{2,1,0:T(2,128)(2,1)}), bf16[8,2,36864]{2,1,0:T(2,128)(2,1)S(1)}, u32[]{:S(2)}, u32[]{:S(2)}) async-start(bf16[8,2,36864]{2,1,0:T(2,128)(2,1)} %reshape.125), calls=%async_computation | async-start | bytes 2359296 | tf_op jit(solution)/shard_map/all_to_all | solution.py:79
  53.1 6.0 %copy-start.1 = (s32[16]{0:T(128)S(1)}, s32[16]{0:T(128)}, u32[]{:S(2)}) copy-start(s32[16]{0:T(128)} %param.8) | copy-start | bytes 196
  55.4 23.4 %all-to-all-start.1 = ((bf16[3,1,384,512]{2,0,1,3:T(4,128)(2,1)}), bf16[3,1,384,512]{2,0,1,3:T(4,128)(2,1)S(1)}, u32[]{:S(2)}, u32[]{:S(2)}) async-start(bf16[3,1,384,512]{2,0,1,3:T(4,128)(2,1)} %copy.62), calls=%async_computation.1 | async-start | bytes 3145728 | tf_op jit(solution)/shard_map/all_to_all | solution.py:78
  58.9 24.3 %copy-start.2 = (s32[20]{0:T(128)S(1)}, s32[20]{0:T(128)}, u32[]{:S(2)}) copy-start(s32[20]{0:T(128)} %constant.115) | copy-start | bytes 244
  79.1 16.6 %collective-permute-start = (bf16[2,4,384,128]{2,3,1,0:T(8,128)(2,1)S(1)}, bf16[2,4,384,128]{2,3,1,0:T(8,128)(2,1)}, u32[]{:S(2)}, u32[]{:S(2)}) collective-permute-start(bf16[2,4,384,128]{2,3,1,0:T(8,128)(2,1)S(1)} %slice_bitcast_fusion), channel_id=1, source_target_pairs={{0,32},{32,64},{64,96},{96,128},{128,160},{160,192},{192,224},{224... | collective-permute-start | bytes 2359304 | tf_op jit(solution)/shard_map/ppermute | solution.py:15
  81.9 19.1 %collective-permute-start.1 = (bf16[2,4,384,128]{2,3,1,0:T(8,128)(2,1)S(1)}, bf16[2,4,384,128]{2,3,1,0:T(8,128)(2,1)S(1)}, u32[]{:S(2)}, u32[]{:S(2)}) collective-permute-start(bf16[2,4,384,128]{2,3,1,0:T(8,128)(2,1)S(1)} %slice_bitcast_fusion), channel_id=1, source_target_pairs={{32,0},{64,32},{96,64},{128,96},{160,128},{192,160},{224,192},{256... | collective-permute-start | bytes 2359304 | tf_op jit(solution)/shard_map/ppermute | solution.py:15
where the time goes:
time: 164 us; the launch traced here: 163 us
  local copies, waits for them, and re-layouts  50.7 us (31%)
  waiting for transfers between devices  49.6 us (30%)
  blocking collectives  22.7 us (14%)
  starting transfers between devices  17.4 us (11%)
  matrix products  16.8 us (10%)
  other arithmetic  5.47 us (3%)
    unnamed x14, local copies, waits for them, and re-layouts  25.4 us
    all_to_all x1, waiting for transfers between devices, on_device(): lax.all_to_all(lax.all_to_all(qkv, 'head', split_axis=3, concat_axis=2, t...  19.4 us
    all_to_all x1, waiting for transfers between devices, on_device(): lax.all_to_all(qkv, 'head', split_axis=3, concat_axis=2, tiled=True)  16.3 us
    ppermute x2, waiting for transfers between devices, passed_along(): return lax.ppermute(value, axis, pairs)  13.9 us
    all_to_all x1, blocking collectives, on_device(): lax.all_to_all(shaped, 'head', split_axis=1, concat_axis=2, tiled=True)  13.2 us
    all_to_all x1, starting transfers between devices, on_device(): lax.all_to_all(qkv, 'head', split_axis=3, concat_axis=2, tiled=True)  10.3 us
    dot_general x4, matrix products, attend(): mixed_out = jnp.dot(shares, value_rows, preferred_element_type=jnp.float32)  9.84 us
    all_to_all x1, blocking collectives, on_device(): lax.all_to_all(lax.all_to_all(shaped, 'head', split_axis=1, concat_axis=2...  9.58 us
  transfers between devices with their start and end apart: 4, of which 4 were waited for; matrix products, arithmetic and copies ran while one was open for 3% of the time, Pallas kernels for 0%

commit v1 on v0

v1 whole, which is shorter than its diff:
```python
import functools
import math

import jax
import jax.numpy as jnp
from jax import lax
from jax.experimental import pallas as pl
from jax.experimental.pallas import tpu as pltpu
from jax.sharding import PartitionSpec as P

HEAD_DIM = 128
BLOCKED = -1e30
PLANE = ("seq", "head")


def swap_pairs(value, axis, first):
    length = lax.axis_size(axis)
    pairs = []
    for low in range(first, length - 1, 2):
        pairs += [(low, low + 1), (low + 1, low)]
    return lax.ppermute(value, axis, pairs)


def to_blocks(rows, parts):
    split = rows.reshape(*rows.shape[:-1], parts, rows.shape[-1] // parts)
    return jnp.moveaxis(split, -2, 0)


def spread(blocks):
    return lax.all_to_all(blocks, PLANE, split_axis=0, concat_axis=0, tiled=True)


def attend_kernel(slab_ref, pattern_ref, counts_ref, q_ref, own_ref, even_ref, odd_ref, out_ref):
    tiles, pieces, piece, width = q_ref.shape
    tile_len = pieces * piece
    slab_total = counts_ref.shape[0]
    scale = math.log2(math.e) / math.sqrt(HEAD_DIM)
    slab = slab_ref[0]
    here = counts_ref[slab]
    even_slab = slab + 1 - 2 * lax.rem(slab, 2)
    odd_slab = slab - 1 + 2 * lax.rem(slab, 2)

    def live_in(other):
        count = counts_ref[jnp.clip(other, 0, slab_total - 1)]
        return jnp.where((other >= 0) & (other < slab_total), count, 0)

    even_count, odd_count = live_in(even_slab), live_in(odd_slab)
    even_column = jnp.where(even_slab < slab, 3, 4)
    odd_column = jnp.where(odd_slab < slab, 3, 4)

    for tile in range(tiles):
        live = tile < here
        asked = [(own_ref, tile, live)]
        if tile >= 1:
            asked.append((own_ref, tile - 1, (pattern_ref[tile, 1] == 1) & (tile - 1 < here)))
        if tile + 1 < tiles:
            asked.append((own_ref, tile + 1, (pattern_ref[tile, 2] == 1) & (tile + 1 < here)))
        asked.append((even_ref, tile, (pattern_ref[tile, even_column] == 1) & (tile < even_count)))
        asked.append((odd_ref, tile, (pattern_ref[tile, odd_column] == 1) & (tile < odd_count)))

        @pl.when(live)
        def _():
            query = q_ref[tile].reshape(tile_len, width)
            scores, peaks, biases = [], [], []
            for ref, place, allowed in asked:
                key = ref[place, :, 0].reshape(tile_len, width)
                score = lax.dot_general(
                    query, key, (((1,), (1,)), ((), ())), preferred_element_type=jnp.float32
                )
                bias = jnp.where(allowed, 0.0, BLOCKED)
                scores.append(score)
                biases.append(bias)
                peaks.append(jnp.max(score, axis=1, keepdims=True) + bias)
            peak = functools.reduce(jnp.maximum, peaks)
            total = jnp.zeros((tile_len, 1), jnp.float32)
            mixed = jnp.zeros((tile_len, width), jnp.float32)
            for score, bias, (ref, place, _) in zip(scores, biases, asked):
                weight = jnp.exp2(score * scale + (bias - peak) * scale)
                total += jnp.sum(weight, axis=1, keepdims=True)
                value = ref[place, :, 1].reshape(tile_len, width)
                mixed += jnp.dot(
                    weight.astype(jnp.bfloat16), value, preferred_element_type=jnp.float32
                )
            out_ref[tile] = (mixed / total).astype(jnp.bfloat16).reshape(pieces, piece, width)

        @pl.when(jnp.logical_not(live))
        def _():
            out_ref[tile] = jnp.zeros((pieces, piece, width), jnp.bfloat16)


def on_device(qkv, pattern, counts):
    seq_count, head_count = lax.axis_size("seq"), lax.axis_size("head")
    parts = seq_count * head_count
    piece, features = qkv.shape[2], qkv.shape[3]
    width = features // parts
    own = spread(to_blocks(qkv[1:3, 0], parts))
    own, raw_query = lax.optimization_barrier((own, qkv[0, 0]))
    own = own.reshape(seq_count, head_count, 2, piece, width)
    even = swap_pairs(own, "slab", 0)
    odd = swap_pairs(own, "slab", 1)
    query = spread(to_blocks(raw_query, parts)).reshape(seq_count, head_count, piece, width)
    slab = lax.axis_index("slab").astype(jnp.int32).reshape(1)
    smem = pl.BlockSpec(memory_space=pltpu.SMEM)
    vmem = pl.BlockSpec(memory_space=pltpu.VMEM)
    pairs = seq_count * 5 * (head_count * piece) ** 2
    attended = pl.pallas_call(
        attend_kernel,
        out_shape=jax.ShapeDtypeStruct(query.shape, jnp.bfloat16),
        in_specs=[smem] * 3 + [vmem] * 4,
        out_specs=vmem,
        compiler_params=pltpu.CompilerParams(vmem_limit_bytes=48 * 2**20),
        cost_estimate=pl.CostEstimate(
            flops=4 * width * pairs, bytes_accessed=8 * query.size * 2, transcendentals=pairs
        ),
    )(slab, pattern, counts, query, own, even, odd)
    returned = spread(attended.reshape(parts, piece, width))
    return jnp.moveaxis(returned, 0, 1).reshape(1, piece, features)


def solution(mesh):
    in_specs = (P(None, ("slab", "seq"), "head", None), P("slab", None), P())
    out_specs = P(("slab", "seq"), "head", None)
    return jax.shard_map(
        on_device, mesh=mesh, in_specs=in_specs, out_specs=out_specs, check_vma=False
    )
```

time: 164 us -> 71.9 us (0.44)
  local copies, waits for them, and re-layouts: 50.7 us -> 4.35 us
  waiting for transfers between devices: 49.6 us -> 26.8 us
  matrix products: 16.8 us -> 0 us
  blocking collectives: 22.7 us -> 14.3 us
  Pallas kernels: 0 us -> 5.92 us
  other arithmetic: 5.47 us -> 0 us
  starting transfers between devices: 17.4 us -> 20.1 us
    unnamed x14 -> x7, local copies, waits for them, and re-layouts: 25.4 us -> 0.17 us
    dot_general x8 -> x0, matrix products: 16.8 us -> none  [the longest x4 9.84 us: attend(): mixed_out = jnp.dot(shares, value_rows, preferred_element_type=jnp.float32)]
    ppermute x2, waiting for transfers between devices: 13.9 us -> 2.25 us  [swap_pairs(): return lax.ppermute(value, axis, pairs)]
    all_to_all x2, waiting for transfers between devices: 35.7 us -> 24.6 us  [spread(): lax.all_to_all(blocks, PLANE, split_axis=0, concat_axis=0, tiled=True)]
    all_to_all x2 -> x1, blocking collectives: 22.7 us -> 14.3 us  [spread(): lax.all_to_all(blocks, PLANE, split_axis=0, concat_axis=0, tiled=True)]
    all_to_all x5 -> x0, local copies, waits for them, and re-layouts: 8.39 us -> none  [the longest x2 7.67 us: on_device(): lax.all_to_all(qkv, 'head', split_axis=3, concat_axis=2, tiled=True)]
    pallas_call x0 -> x1, Pallas kernels: none -> 5.92 us  [on_device(): pl.pallas_call(attend_kernel, out_shape=jax.ShapeDtypeStruct(query.shape,...]
    transpose x1 -> x2, local copies, waits for them, and re-layouts: 6.26 us -> 0.92 us  [the longest x1 0.81 us: to_blocks(): return jnp.moveaxis(split, -2, 0)]
  transfers between devices with their start and end apart: 4 -> 4, of which waited for: 4 -> 3; matrix products, arithmetic and copies ran while one was open for 3% -> 1% of each run, Pallas kernels for 0% -> 0%
where the time goes in v1:
time: 71.9 us; the launch traced here: 71.5 us
  waiting for transfers between devices  26.8 us (37%)
  starting transfers between devices  20.1 us (28%)
  blocking collectives  14.3 us (20%)
  Pallas kernels  5.92 us (8%)
  local copies, waits for them, and re-layouts  4.35 us (6%)
    all_to_all x2, waiting for transfers between devices, spread(): lax.all_to_all(blocks, PLANE, split_axis=0, concat_axis=0, tiled=True)  24.6 us
    all_to_all x2, starting transfers between devices, spread(): lax.all_to_all(blocks, PLANE, split_axis=0, concat_axis=0, tiled=True)  15 us
    all_to_all x1, blocking collectives, spread(): lax.all_to_all(blocks, PLANE, split_axis=0, concat_axis=0, tiled=True)  14.3 us
    pallas_call x1, Pallas kernels, on_device(): pl.pallas_call(attend_kernel, out_shape=jax.ShapeDtypeStruct(query.shape,...  5.92 us
    ppermute x2, starting transfers between devices, swap_pairs(): return lax.ppermute(value, axis, pairs)  5.12 us
    ppermute x2, waiting for transfers between devices, swap_pairs(): return lax.ppermute(value, axis, pairs)  2.25 us
  transfers between devices with their start and end apart: 4, of which 3 were waited for; matrix products, arithmetic and copies ran while one was open for 1% of the time, Pallas kernels for 0%

profile of v1, /device:TPU:1, one launch (start us, length us, event | category | flops | bytes accessed | tf_op | source)
XLA Modules:
  0.0 71.5 jit_solution(7887802460157012640)
XLA Ops:
  0.0 0.0 slice-start
  0.0 1.1 %slice-done = bf16[2,1,48,4096]{3,2,1,0:T(8,128)(2,1)S(1)} async-done(((bf16[3,1,48,4096]{3,2,1,0:T(8,128)(2,1)}), bf16[2,1,48,4096]{3,2,1,0:T(8,128)(2,1)S(1)}, s32[]{:S(2)}) %slice-start) | async-done | bytes 786456 | tf_op jit(solution)/shard_map/slice | solution.py:96
  1.1 0.2 copy.8
  1.3 1.2 %copy.11 = bf16[2,48,32,128]{3,1,0,2:T(8,128)(2,1)} copy(bf16[2,48,32,128]{3,2,1,0:T(8,128)(2,1)S(1)} %bitcast.27) | data formatting | bytes 1572864 | tf_op jit(solution)/shard_map/reshape;squeeze | solution.py:25
  2.5 0.0 copy-start.2
  2.5 10.6 %all-to-all-start = ((bf16[32,2,48,128]{3,2,1,0:T(8,128)(2,1)}), bf16[32,2,48,128]{3,2,1,0:T(8,128)(2,1)S(1)}, u32[]{:S(2)}, u32[]{:S(2)}) async-start(bf16[32,2,48,128]{3,2,1,0:T(8,128)(2,1)} %bitcast.21), calls=%async_computation | async-start | bytes 1572864 | tf_op jit(solution)/shard_map/all_to_all | solution.py:30
  13.1 0.0 copy-done.2
  13.1 0.0 copy-start
  13.1 0.0 copy-start.1
  13.1 14.3 %all-to-all-done = bf16[32,2,48,128]{3,2,1,0:T(8,128)(2,1)S(1)} async-done(((bf16[32,2,48,128]{3,2,1,0:T(8,128)(2,1)}), bf16[32,2,48,128]{3,2,1,0:T(8,128)(2,1)S(1)}, u32[]{:S(2)}, u32[]{:S(2)}) %all-to-all-start) | async-done | bytes 786464 | tf_op jit(solution)/shard_map/all_to_all | solution.py:30
  27.4 0.7 collective-permute-start.1
  28.1 4.4 %collective-permute-start = (bf16[4,8,2,48,128]{4,3,2,1,0:T(8,128)(2,1)S(1)}, bf16[4,8,2,48,128]{4,3,2,1,0:T(8,128)(2,1)S(1)}, u32[]{:S(2)}, u32[]{:S(2)}) collective-permute-start(bf16[4,8,2,48,128]{4,3,2,1,0:T(8,128)(2,1)S(1)} %bitcast.23), channel_id=1, source_target_pairs={{0,32},{32,0},{64,96},{96,64},{128,160},{160,128},{192,224},{224,1... | collective-permute-start | bytes 2359304 | tf_op jit(solution)/shard_map/ppermute | solution.py:21
  32.5 0.8 %bitcast_bitcast_fusion = bf16[32,48,128]{2,1,0:T(8,128)(2,1)} fusion(bf16[48,4096]{1,0:T(8,128)(2,1)S(1)} %slice_bitcast_fusion), kind=kLoop, calls=%fused_computation.1 | loop fusion | bytes 786432 | tf_op jit(solution)/shard_map/transpose | solution.py:26
  33.3 4.4 %all-to-all-start.1 = ((bf16[32,48,128]{2,1,0:T(8,128)(2,1)}), bf16[32,48,128]{2,1,0:T(8,128)(2,1)S(1)}, u32[]{:S(2)}, u32[]{:S(2)}) async-start(bf16[32,48,128]{2,1,0:T(8,128)(2,1)} %bitcast_bitcast_fusion), calls=%async_computation.1 | async-start | bytes 786432 | tf_op jit(solution)/shard_map/all_to_all | solution.py:30
  37.8 10.3 %all-to-all-done.1 = bf16[32,48,128]{2,1,0:T(8,128)(2,1)S(1)} async-done(((bf16[32,48,128]{2,1,0:T(8,128)(2,1)}), bf16[32,48,128]{2,1,0:T(8,128)(2,1)S(1)}, u32[]{:S(2)}, u32[]{:S(2)}) %all-to-all-start.1) | async-done | bytes 393248 | tf_op jit(solution)/shard_map/all_to_all | solution.py:30
  48.1 0.0 collective-permute-done.1.odd_ref
  48.1 2.2 %collective-permute-done.even_ref = bf16[4,8,2,48,128]{4,3,2,1,0:T(8,128)(2,1)S(1)} collective-permute-done((bf16[4,8,2,48,128]{4,3,2,1,0:T(8,128)(2,1)S(1)}, bf16[4,8,2,48,128]{4,3,2,1,0:T(8,128)(2,1)S(1)}, u32[]{:S(2)}, u32[]{:S(2)}) %collective-permute-start) | collective-permute-done | bytes 786464 | tf_op jit(solution)/shard_map/ppermute | solution.py:21
  50.3 0.0 copy-done
  50.3 0.0 copy-done.1
  50.3 5.9 %shard_map.37 = bf16[4,8,48,128]{3,2,1,0:T(8,128)(2,1)S(1)} custom-call(s32[1]{0:T(128)} %bitcast.slab_ref, s32[4,5]{1,0:T(4,128)S(1)} %copy-done, s32[16]{0:T(128)S(1)} %copy-done.1, bf16[4,8,48,128]{3,2,1,0:T(8,128)(2,1)S(1)} %bitcast.25, bf16[4,8,2,48,128]{4,3,2,1,0:T(8,128)(2,1)S(1)} %bitcast.24, ...), custom_call_target="tpu_custom_call" | custom-call | flops 1509949440 | bytes 3145728 | tf_op jit(solution)/shard_map/pallas_call | solution.py:106
  56.2 14.3 %all_to_all.15 = bf16[32,48,128]{2,1,0:T(8,128)(2,1)S(1)} all-to-all(bf16[32,48,128]{2,1,0:T(8,128)(2,1)S(1)} %bitcast.26), channel_id=1, replica_groups=mesh['slab'=16,'head'=8,'seq'=4] {'seq','head'}, dimensions={0} | all-to-all | bytes 786432 | tf_op jit(solution)/shard_map/all_to_all | solution.py:30
  70.5 0.1 copy.6
  70.6 0.9 %reshape.23 = bf16[1,48,4096]{2,1,0:T(8,128)(2,1)} reshape(bf16[48,32,128]{2,1,0:T(8,128)(2,1)S(1)} %copy.6) | data formatting | bytes 786432 | tf_op jit(solution)/shard_map/reshape | solution.py:117
  (1 shorter events, 0.0 us)
Async XLA Ops:
  0.0 1.1 %slice-start = ((bf16[3,1,48,4096]{3,2,1,0:T(8,128)(2,1)}), bf16[2,1,48,4096]{3,2,1,0:T(8,128)(2,1)S(1)}, s32[]{:S(2)}) async-start(bf16[3,1,48,4096]{3,2,1,0:T(8,128)(2,1)} %param.3), calls=%async_computation.3 | async-start | bytes 1572864 | tf_op jit(solution)/shard_map/slice | solution.py:96
  2.5 10.6 %copy-start.2 = (bf16[3,1,48,4096]{3,2,1,0:T(8,128)(2,1)S(1)}, bf16[3,1,48,4096]{3,2,1,0:T(8,128)(2,1)}, u32[]{:S(2)}) copy-start(bf16[3,1,48,4096]{3,2,1,0:T(8,128)(2,1)} %param.3) | copy-start | bytes 3538948
  2.5 24.9 %all-to-all-start = ((bf16[32,2,48,128]{3,2,1,0:T(8,128)(2,1)}), bf16[32,2,48,128]{3,2,1,0:T(8,128)(2,1)S(1)}, u32[]{:S(2)}, u32[]{:S(2)}) async-start(bf16[32,2,48,128]{3,2,1,0:T(8,128)(2,1)} %bitcast.21), calls=%async_computation | async-start | bytes 1572864 | tf_op jit(solution)/shard_map/all_to_all | solution.py:30
  13.1 37.2 %copy-start = (s32[4,5]{1,0:T(4,128)S(1)}, s32[4,5]{1,0:T(4,128)}, u32[]{:S(2)}) copy-start(s32[4,5]{1,0:T(4,128)} %pattern_ref.1) | copy-start | bytes 244
  13.1 37.2 %copy-start.1 = (s32[16]{0:T(128)S(1)}, s32[16]{0:T(128)}, u32[]{:S(2)}) copy-start(s32[16]{0:T(128)} %counts_ref.1) | copy-start | bytes 196
  27.4 20.7 %collective-permute-start.1 = (bf16[4,8,2,48,128]{4,3,2,1,0:T(8,128)(2,1)S(1)}, bf16[4,8,2,48,128]{4,3,2,1,0:T(8,128)(2,1)S(1)}, u32[]{:S(2)}, u32[]{:S(2)}) collective-permute-start(bf16[4,8,2,48,128]{4,3,2,1,0:T(8,128)(2,1)S(1)} %bitcast.22), channel_id=1, source_target_pairs={{32,64},{64,32},{96,128},{128,96},{160,192},{192,160},{224,256},{2... | collective-permute-start | bytes 2359304 | tf_op jit(solution)/shard_map/ppermute | solution.py:21
  28.1 22.2 %collective-permute-start = (bf16[4,8,2,48,128]{4,3,2,1,0:T(8,128)(2,1)S(1)}, bf16[4,8,2,48,128]{4,3,2,1,0:T(8,128)(2,1)S(1)}, u32[]{:S(2)}, u32[]{:S(2)}) collective-permute-start(bf16[4,8,2,48,128]{4,3,2,1,0:T(8,128)(2,1)S(1)} %bitcast.23), channel_id=1, source_target_pairs={{0,32},{32,0},{64,96},{96,64},{128,160},{160,128},{192,224},{224,1... | collective-permute-start | bytes 2359304 | tf_op jit(solution)/shard_map/ppermute | solution.py:21
  33.3 14.7 %all-to-all-start.1 = ((bf16[32,48,128]{2,1,0:T(8,128)(2,1)}), bf16[32,48,128]{2,1,0:T(8,128)(2,1)S(1)}, u32[]{:S(2)}, u32[]{:S(2)}) async-start(bf16[32,48,128]{2,1,0:T(8,128)(2,1)} %bitcast_bitcast_fusion), calls=%async_computation.1 | async-start | bytes 786432 | tf_op jit(solution)/shard_map/all_to_all | solution.py:30

commit v2 on v1

v2 whole, which is shorter than its diff:
```python
import functools
import math

import jax
import jax.numpy as jnp
from jax import lax
from jax.experimental import pallas as pl
from jax.experimental.pallas import tpu as pltpu
from jax.sharding import PartitionSpec as P

HEAD_DIM = 128
BLOCKED = -1e30
SCALE = math.log2(math.e) / math.sqrt(HEAD_DIM)
SMEM = pl.BlockSpec(memory_space=pltpu.SMEM)
VMEM = pl.BlockSpec(memory_space=pltpu.VMEM)
PARAMS = pltpu.CompilerParams(vmem_limit_bytes=40 * 2**20)


def passed_along(value, axis, even_by):
    length, heads = lax.axis_size(axis), lax.axis_size("head")
    outer = axis == "slab"
    pairs = []
    for place in range(length):
        for head in range(heads):
            target = place + (even_by if head % 2 == 0 else -even_by)
            if 0 <= target < length:
                if outer:
                    pairs.append((place * heads + head, target * heads + head))
                else:
                    pairs.append((head * length + place, head * length + target))
    return lax.ppermute(value, (axis, "head") if outer else ("head", axis), pairs)


def spread(blocks):
    return lax.all_to_all(blocks, "head", split_axis=0, concat_axis=0, tiled=True)


def to_blocks_kernel(rows_ref, blocks_ref):
    parts, arrays, _, width = blocks_ref.shape
    for array in range(arrays):
        for part in range(parts):
            columns = slice(part * width, (part + 1) * width)
            blocks_ref[part, array] = rows_ref[array, 0, :, columns]


def to_blocks(rows, parts):
    arrays, _, tokens, features = rows.shape
    return pl.pallas_call(
        to_blocks_kernel,
        out_shape=jax.ShapeDtypeStruct((parts, arrays, tokens, features // parts), rows.dtype),
        in_specs=[VMEM],
        out_specs=VMEM,
        compiler_params=PARAMS,
        cost_estimate=pl.CostEstimate(flops=0, bytes_accessed=4 * rows.size, transcendentals=0),
    )(rows)


def to_rows_kernel(blocks_ref, rows_ref):
    parts, _, width = blocks_ref.shape
    for part in range(parts):
        rows_ref[0, :, part * width : (part + 1) * width] = blocks_ref[part]


def to_rows(blocks):
    parts, tokens, width = blocks.shape
    return pl.pallas_call(
        to_rows_kernel,
        out_shape=jax.ShapeDtypeStruct((1, tokens, parts * width), blocks.dtype),
        in_specs=[VMEM],
        out_specs=VMEM,
        compiler_params=PARAMS,
        cost_estimate=pl.CostEstimate(flops=0, bytes_accessed=4 * blocks.size, transcendentals=0),
    )(blocks)


def columns_of(ref, which, head):
    pieces, _, piece, _ = ref.shape
    columns = slice(head * HEAD_DIM, (head + 1) * HEAD_DIM)
    return ref[:, which, :, columns].reshape(pieces * piece, HEAD_DIM)


def attend_kernel(place_ref, pattern_ref, counts_ref, q_ref, own_ref, x1_ref, z1_ref, x0_ref, z0_ref, out_ref):
    pieces, _, piece, width = q_ref.shape
    tile_len = pieces * piece
    last = counts_ref.shape[0] - 1
    slab, slot, core = place_ref[0], place_ref[1], place_ref[2]
    here = counts_ref[slab]
    below = jnp.where(slab >= 1, counts_ref[jnp.maximum(slab - 1, 0)], 0)
    above = jnp.where(slab < last, counts_ref[jnp.minimum(slab + 1, last)], 0)
    wants = [pattern_ref[slot, column] == 1 for column in range(5)]
    left = wants[1] & (slot >= 1)
    right = wants[2] & (slot + 1 < here)
    down = wants[3] & (slot < below)
    up = wants[4] & (slot < above)
    even = core == 0
    asked = [
        (own_ref, True),
        (x0_ref, (even & left) | (~even & right)),
        (x1_ref, (even & right) | (~even & left)),
        (z0_ref, (even & down) | (~even & up)),
        (z1_ref, (even & up) | (~even & down)),
    ]
    biases = [jnp.where(allowed, 0.0, BLOCKED) for _, allowed in asked]

    @pl.when(slot < here)
    def _():
        for head in range(width // HEAD_DIM):
            query = columns_of(q_ref, 0, head)
            scores = [
                lax.dot_general(
                    query,
                    columns_of(ref, 0, head),
                    (((1,), (1,)), ((), ())),
                    preferred_element_type=jnp.float32,
                )
                for ref, _ in asked
            ]
            tops = [
                functools.reduce(
                    jnp.maximum, [score[:, k : k + 128] for k in range(0, tile_len, 128)]
                )
                + bias
                for score, bias in zip(scores, biases)
            ]
            peak = jnp.max(functools.reduce(jnp.maximum, tops), axis=1, keepdims=True)
            total, mixed = 0.0, 0.0
            for score, bias, (ref, _) in zip(scores, biases, asked):
                weight = jnp.exp2(score * SCALE + (bias - peak) * SCALE)
                total += functools.reduce(
                    jnp.add, [weight[:, k : k + 128] for k in range(0, tile_len, 128)]
                )
                mixed += jnp.dot(
                    weight.astype(jnp.bfloat16),
                    columns_of(ref, 1, head),
                    preferred_element_type=jnp.float32,
                )
            mixed = mixed / jnp.sum(total, axis=1, keepdims=True)
            out_ref[:, :, head * HEAD_DIM : (head + 1) * HEAD_DIM] = mixed.astype(
                jnp.bfloat16
            ).reshape(pieces, piece, HEAD_DIM)

    @pl.when(slot >= here)
    def _():
        out_ref[...] = jnp.zeros(out_ref.shape, jnp.bfloat16)


def on_device(qkv, pattern, counts):
    parts = lax.axis_size("head")
    piece, features = qkv.shape[2], qkv.shape[3]
    width = features // parts
    place = jnp.stack(
        [lax.axis_index("slab"), lax.axis_index("seq"), lax.axis_index("head") % 2]
    ).astype(jnp.int32)
    own = spread(to_blocks(qkv[1:3], parts))
    own, raw_query = lax.optimization_barrier((own, to_blocks(qkv[:1], parts)))
    z0 = passed_along(own, "slab", 1)
    x0 = passed_along(own, "seq", 1)
    z1 = passed_along(own, "slab", -1)
    x1 = passed_along(own, "seq", -1)
    query = spread(raw_query)
    attended = pl.pallas_call(
        attend_kernel,
        out_shape=jax.ShapeDtypeStruct((parts, piece, width), jnp.bfloat16),
        in_specs=[SMEM] * 3 + [VMEM] * 6,
        out_specs=VMEM,
        compiler_params=PARAMS,
        cost_estimate=pl.CostEstimate(
            flops=1500000000, bytes_accessed=2**22, transcendentals=2949120
        ),
    )(place, pattern, counts, query, own, x1, z1, x0, z0)
    return to_rows(spread(attended))


def solution(mesh):
    in_specs = (P(None, ("slab", "seq"), "head", None), P("slab", None), P())
    out_specs = P(("slab", "seq"), "head", None)
    return jax.shard_map(
        on_device, mesh=mesh, in_specs=in_specs, out_specs=out_specs, check_vma=False
    )
```

time: 71.9 us -> 66 us (0.918)
  waiting for transfers between devices: 26.8 us -> 17.6 us
  starting transfers between devices: 20.1 us -> 25.2 us
  Pallas kernels: 5.92 us -> 8.72 us
  blocking collectives: 14.3 us -> 11.5 us
  local copies, waits for them, and re-layouts: 4.35 us -> 2.24 us
    all_to_all x2, waiting for transfers between devices: 24.6 us -> 17.6 us  [spread(): lax.all_to_all(blocks, 'head', split_axis=0, concat_axis=0, tiled=True)]
    ppermute x2 -> x4, starting transfers between devices: 5.12 us -> 11.5 us  [passed_along(): lax.ppermute(value, (axis, 'head') if outer else ('head', axis), pairs)]
    pallas_call x1 -> x4, Pallas kernels: 5.92 us -> 8.72 us  [the longest x1 6.24 us: on_device(): pl.pallas_call(attend_kernel, out_shape=jax.ShapeDtypeStruct((parts, piec...]
    all_to_all x1, blocking collectives: 14.3 us -> 11.5 us  [spread(): lax.all_to_all(blocks, 'head', split_axis=0, concat_axis=0, tiled=True)]
    ppermute x2 -> x4, waiting for transfers between devices: 2.25 us -> 0.01 us  [passed_along(): lax.ppermute(value, (axis, 'head') if outer else ('head', axis), pairs)]
    all_to_all x2, starting transfers between devices: 15 us -> 13.7 us  [spread(): lax.all_to_all(blocks, 'head', split_axis=0, concat_axis=0, tiled=True)]
    another operation x1 -> x0, local copies, waits for them, and re-layouts: 1.19 us -> none  [to_blocks(): split = rows.reshape(*rows.shape[:-1], parts, rows.shape[-1] // parts)]
    slice x2, local copies, waits for them, and re-layouts: 1.13 us -> 2.23 us  [the longest x1 1.18 us: on_device(): own = spread(to_blocks(qkv[1:3], parts))]
  transfers between devices with their start and end apart: 4 -> 6, of which waited for: 3 -> 2; matrix products, arithmetic and copies ran while one was open for 1% -> 2% of each run, Pallas kernels for 0% -> 1%
where the time goes in v2:
time: 66 us; the launch traced here: 65.5 us
  starting transfers between devices  25.2 us (38%)
  waiting for transfers between devices  17.6 us (27%)
  blocking collectives  11.5 us (17%)
  Pallas kernels  8.72 us (13%)
  local copies, waits for them, and re-layouts  2.24 us (3%)
    all_to_all x2, waiting for transfers between devices, spread(): lax.all_to_all(blocks, 'head', split_axis=0, concat_axis=0, tiled=True)  17.6 us
    all_to_all x2, starting transfers between devices, spread(): lax.all_to_all(blocks, 'head', split_axis=0, concat_axis=0, tiled=True)  13.7 us
    all_to_all x1, blocking collectives, spread(): lax.all_to_all(blocks, 'head', split_axis=0, concat_axis=0, tiled=True)  11.5 us
    ppermute x4, starting transfers between devices, passed_along(): lax.ppermute(value, (axis, 'head') if outer else ('head', axis), pairs)  11.5 us
    pallas_call x1, Pallas kernels, on_device(): pl.pallas_call(attend_kernel, out_shape=jax.ShapeDtypeStruct((parts, piec...  6.24 us
    pallas_call x2, Pallas kernels, to_blocks(): pl.pallas_call(to_blocks_kernel, out_shape=jax.ShapeDtypeStruct((parts, a...  1.71 us
  transfers between devices with their start and end apart: 6, of which 2 were waited for; matrix products, arithmetic and copies ran while one was open for 2% of the time, Pallas kernels for 1%

profile of v2, /device:TPU:1, one launch (start us, length us, event | category | flops | bytes accessed | tf_op | source)
XLA Modules:
  0.0 65.5 jit_solution(6721098462225606050)
XLA Ops:
  0.0 1.2 %slice.6.rows_ref = bf16[2,1,48,4096]{3,2,1,0:T(8,128)(2,1)S(1)} slice(bf16[3,1,48,4096]{3,2,1,0:T(8,128)(2,1)} %param.3), slice={[1:3], [0:1], [0:48], [0:4096]} | slice | bytes 1572864 | tf_op jit(solution)/shard_map/slice | solution.py:154
  1.2 0.9 %shard_map.37 = bf16[8,2,48,512]{3,2,1,0:T(8,128)(2,1)} custom-call(bf16[2,1,48,4096]{3,2,1,0:T(8,128)(2,1)S(1)} %slice.6.rows_ref), custom_call_target="tpu_custom_call" | custom-call | bytes 1572864 | tf_op jit(solution)/shard_map/pallas_call | solution.py:48
  2.1 10.3 %all-to-all-start = ((bf16[8,2,48,512]{3,2,1,0:T(8,128)(2,1)}), bf16[8,2,48,512]{3,2,1,0:T(8,128)(2,1)S(1)}, u32[]{:S(2)}, u32[]{:S(2)}) async-start(bf16[8,2,48,512]{3,2,1,0:T(8,128)(2,1)} %shard_map.37), calls=%async_computation | async-start | bytes 1572864 | tf_op jit(solution)/shard_map/all_to_all | solution.py:35
  12.4 0.0 copy-start
  12.4 0.0 copy-start.1
  12.5 1.0 %slice.7.rows_ref = bf16[1,1,48,4096]{3,2,1,0:T(8,128)(2,1)S(1)} slice(bf16[3,1,48,4096]{3,2,1,0:T(8,128)(2,1)} %param.3), slice={[0:1], [0:1], [0:48], [0:4096]} | slice | bytes 786432 | tf_op jit(solution)/shard_map/slice | solution.py:155
  13.5 0.8 %shard_map.38 = bf16[8,1,48,512]{3,2,1,0:T(8,128)(2,1)} custom-call(bf16[1,1,48,4096]{3,2,1,0:T(8,128)(2,1)S(1)} %slice.7.rows_ref), custom_call_target="tpu_custom_call" | custom-call | bytes 786432 | tf_op jit(solution)/shard_map/pallas_call | solution.py:48
  14.3 10.5 %all-to-all-done.own_ref = bf16[8,2,48,512]{3,2,1,0:T(8,128)(2,1)S(1)} async-done(((bf16[8,2,48,512]{3,2,1,0:T(8,128)(2,1)}), bf16[8,2,48,512]{3,2,1,0:T(8,128)(2,1)S(1)}, u32[]{:S(2)}, u32[]{:S(2)}) %all-to-all-start) | async-done | bytes 786464 | tf_op jit(solution)/shard_map/all_to_all | solution.py:35
  24.8 1.3 %collective-permute-start.3 = (bf16[8,2,48,512]{3,2,1,0:T(8,128)(2,1)S(1)}, bf16[8,2,48,512]{3,2,1,0:T(8,128)(2,1)S(1)}, u32[]{:S(2)}, u32[]{:S(2)}) collective-permute-start(bf16[8,2,48,512]{3,2,1,0:T(8,128)(2,1)S(1)} %all-to-all-done.own_ref), channel_id=1, source_target_pairs={{0,32},{8,40},{16,48},{24,56},{32,64},{36,4},{40,72},{44,12},{48,8... | collective-permute-start | bytes 2359304 | tf_op jit(solution)/shard_map/ppermute | solution.py:31
  26.0 1.3 %collective-permute-start.2 = (bf16[8,2,48,512]{3,2,1,0:T(8,128)(2,1)S(1)}, bf16[8,2,48,512]{3,2,1,0:T(8,128)(2,1)S(1)}, u32[]{:S(2)}, u32[]{:S(2)}) collective-permute-start(bf16[8,2,48,512]{3,2,1,0:T(8,128)(2,1)S(1)} %all-to-all-done.own_ref), channel_id=1, source_target_pairs={{0,1},{8,9},{16,17},{24,25},{1,2},{5,4},{9,10},{13,12},{17,18},{21... | collective-permute-start | bytes 2359304 | tf_op jit(solution)/shard_map/ppermute | solution.py:31
  27.3 4.0 %collective-permute-start.1 = (bf16[8,2,48,512]{3,2,1,0:T(8,128)(2,1)S(1)}, bf16[8,2,48,512]{3,2,1,0:T(8,128)(2,1)S(1)}, u32[]{:S(2)}, u32[]{:S(2)}) collective-permute-start(bf16[8,2,48,512]{3,2,1,0:T(8,128)(2,1)S(1)} %all-to-all-done.own_ref), channel_id=1, source_target_pairs={{4,36},{12,44},{20,52},{28,60},{32,0},{36,68},{40,8},{44,76},{48,1... | collective-permute-start | bytes 2359304 | tf_op jit(solution)/shard_map/ppermute | solution.py:31
  31.4 4.9 %collective-permute-start = (bf16[8,2,48,512]{3,2,1,0:T(8,128)(2,1)S(1)}, bf16[8,2,48,512]{3,2,1,0:T(8,128)(2,1)}, u32[]{:S(2)}, u32[]{:S(2)}) collective-permute-start(bf16[8,2,48,512]{3,2,1,0:T(8,128)(2,1)S(1)} %all-to-all-done.own_ref), channel_id=1, source_target_pairs={{4,5},{12,13},{20,21},{28,29},{1,0},{5,6},{9,8},{13,14},{17,16},{2... | collective-permute-start | bytes 2359304 | tf_op jit(solution)/shard_map/ppermute | solution.py:31
  36.3 3.4 %all-to-all-start.1 = ((bf16[8,1,48,512]{3,2,1,0:T(8,128)(2,1)}), bf16[8,1,48,512]{3,2,1,0:T(8,128)(2,1)S(1)}, u32[]{:S(2)}, u32[]{:S(2)}) async-start(bf16[8,1,48,512]{3,2,1,0:T(8,128)(2,1)} %shard_map.38), calls=%async_computation.1 | async-start | bytes 786432 | tf_op jit(solution)/shard_map/all_to_all | solution.py:35
  39.7 0.1 pad_add_fusion.place_ref
  39.8 7.1 %all-to-all-done.1.q_ref = bf16[8,1,48,512]{3,2,1,0:T(8,128)(2,1)S(1)} async-done(((bf16[8,1,48,512]{3,2,1,0:T(8,128)(2,1)}), bf16[8,1,48,512]{3,2,1,0:T(8,128)(2,1)S(1)}, u32[]{:S(2)}, u32[]{:S(2)}) %all-to-all-start.1) | async-done | bytes 393248 | tf_op jit(solution)/shard_map/all_to_all | solution.py:35
  46.9 0.0 collective-permute-done.3.z0_ref
  46.9 0.0 collective-permute-done.2.x0_ref
  46.9 0.0 collective-permute-done.1.z1_ref
  46.9 0.0 collective-permute-done.x1_ref
  46.9 0.0 copy-done
  46.9 0.0 copy-done.1
  46.9 6.2 %shard_map.39 = bf16[8,48,512]{2,1,0:T(8,128)(2,1)S(1)} custom-call(s32[3]{0:T(128)S(1)} %pad_add_fusion.place_ref, s32[4,5]{1,0:T(4,128)S(1)} %copy-done, s32[16]{0:T(128)S(1)} %copy-done.1, bf16[8,1,48,512]{3,2,1,0:T(8,128)(2,1)S(1)} %all-to-all-done.1.q_ref, bf16[8,2,48,512]{3,2,1,0:T(8,128)(2,1)S(1)} %all-to-all-done.own_ref, ...), custom_call_target="tpu_custom_call" | custom-call | flops 1500000000 | bytes 4194304 | tf_op jit(solution)/shard_map/pallas_call | solution.py:161
  53.2 11.5 %all_to_all.15.blocks_ref = bf16[8,48,512]{2,1,0:T(8,128)(2,1)S(1)} all-to-all(bf16[8,48,512]{2,1,0:T(8,128)(2,1)S(1)} %shard_map.39), channel_id=1, replica_groups=mesh['slab'=16,'head'=8,'seq'=4] {'head'}, dimensions={0} | all-to-all | bytes 786432 | tf_op jit(solution)/shard_map/all_to_all | solution.py:35
  64.7 0.8 %shard_map.40 = bf16[1,48,4096]{2,1,0:T(8,128)(2,1)} custom-call(bf16[8,48,512]{2,1,0:T(8,128)(2,1)S(1)} %all_to_all.15.blocks_ref), custom_call_target="tpu_custom_call" | custom-call | bytes 786432 | tf_op jit(solution)/shard_map/pallas_call | solution.py:66
Async XLA Ops:
  2.1 22.6 %all-to-all-start = ((bf16[8,2,48,512]{3,2,1,0:T(8,128)(2,1)}), bf16[8,2,48,512]{3,2,1,0:T(8,128)(2,1)S(1)}, u32[]{:S(2)}, u32[]{:S(2)}) async-start(bf16[8,2,48,512]{3,2,1,0:T(8,128)(2,1)} %shard_map.37), calls=%async_computation | async-start | bytes 1572864 | tf_op jit(solution)/shard_map/all_to_all | solution.py:35
  12.4 34.5 %copy-start = (s32[4,5]{1,0:T(4,128)S(1)}, s32[4,5]{1,0:T(4,128)}, u32[]{:S(2)}) copy-start(s32[4,5]{1,0:T(4,128)} %pattern_ref.1) | copy-start | bytes 244
  12.4 34.5 %copy-start.1 = (s32[16]{0:T(128)S(1)}, s32[16]{0:T(128)}, u32[]{:S(2)}) copy-start(s32[16]{0:T(128)} %counts_ref.1) | copy-start | bytes 196
  24.8 22.1 %collective-permute-start.3 = (bf16[8,2,48,512]{3,2,1,0:T(8,128)(2,1)S(1)}, bf16[8,2,48,512]{3,2,1,0:T(8,128)(2,1)S(1)}, u32[]{:S(2)}, u32[]{:S(2)}) collective-permute-start(bf16[8,2,48,512]{3,2,1,0:T(8,128)(2,1)S(1)} %all-to-all-done.own_ref), channel_id=1, source_target_pairs={{0,32},{8,40},{16,48},{24,56},{32,64},{36,4},{40,72},{44,12},{48,8... | collective-permute-start | bytes 2359304 | tf_op jit(solution)/shard_map/ppermute | solution.py:31
  26.0 20.8 %collective-permute-start.2 = (bf16[8,2,48,512]{3,2,1,0:T(8,128)(2,1)S(1)}, bf16[8,2,48,512]{3,2,1,0:T(8,128)(2,1)S(1)}, u32[]{:S(2)}, u32[]{:S(2)}) collective-permute-start(bf16[8,2,48,512]{3,2,1,0:T(8,128)(2,1)S(1)} %all-to-all-done.own_ref), channel_id=1, source_target_pairs={{0,1},{8,9},{16,17},{24,25},{1,2},{5,4},{9,10},{13,12},{17,18},{21... | collective-permute-start | bytes 2359304 | tf_op jit(solution)/shard_map/ppermute | solution.py:31
  27.3 19.5 %collective-permute-start.1 = (bf16[8,2,48,512]{3,2,1,0:T(8,128)(2,1)S(1)}, bf16[8,2,48,512]{3,2,1,0:T(8,128)(2,1)S(1)}, u32[]{:S(2)}, u32[]{:S(2)}) collective-permute-start(bf16[8,2,48,512]{3,2,1,0:T(8,128)(2,1)S(1)} %all-to-all-done.own_ref), channel_id=1, source_target_pairs={{4,36},{12,44},{20,52},{28,60},{32,0},{36,68},{40,8},{44,76},{48,1... | collective-permute-start | bytes 2359304 | tf_op jit(solution)/shard_map/ppermute | solution.py:31
  31.4 15.5 %collective-permute-start = (bf16[8,2,48,512]{3,2,1,0:T(8,128)(2,1)S(1)}, bf16[8,2,48,512]{3,2,1,0:T(8,128)(2,1)}, u32[]{:S(2)}, u32[]{:S(2)}) collective-permute-start(bf16[8,2,48,512]{3,2,1,0:T(8,128)(2,1)S(1)} %all-to-all-done.own_ref), channel_id=1, source_target_pairs={{4,5},{12,13},{20,21},{28,29},{1,0},{5,6},{9,8},{13,14},{17,16},{2... | collective-permute-start | bytes 2359304 | tf_op jit(solution)/shard_map/ppermute | solution.py:31
  36.3 10.6 %all-to-all-start.1 = ((bf16[8,1,48,512]{3,2,1,0:T(8,128)(2,1)}), bf16[8,1,48,512]{3,2,1,0:T(8,128)(2,1)S(1)}, u32[]{:S(2)}, u32[]{:S(2)}) async-start(bf16[8,1,48,512]{3,2,1,0:T(8,128)(2,1)} %shard_map.38), calls=%async_computation.1 | async-start | bytes 786432 | tf_op jit(solution)/shard_map/all_to_all | solution.py:35

commit v3 on v2

v3 whole, which is shorter than its diff:
```python
import functools
import math

import jax
import jax.numpy as jnp
from jax import lax
from jax.experimental import pallas as pl
from jax.experimental.pallas import tpu as pltpu
from jax.sharding import Mesh
from jax.sharding import PartitionSpec as P

HEAD_DIM = 128
PAIR = ("lane", "head")
SCALE = math.log2(math.e) / math.sqrt(HEAD_DIM)
SMEM = pl.BlockSpec(memory_space=pltpu.SMEM)
VMEM = pl.BlockSpec(memory_space=pltpu.VMEM)
PARAMS = pltpu.CompilerParams(vmem_limit_bytes=40 * 2**20)


def passed_along(value, even_by):
    slabs, heads = lax.axis_size("slab"), lax.axis_size("head")
    moves = []
    for slab in range(slabs):
        for head in range(heads):
            target = slab + (even_by if head % 2 == 0 else -even_by)
            if 0 <= target < slabs:
                moves.append((slab * heads + head, target * heads + head))
    return lax.ppermute(value, ("slab", "head"), moves)


def swapped_across(value):
    return lax.ppermute(value, ("pair", "lane"), [(0, 3), (3, 0), (1, 2), (2, 1)])


def spread(blocks):
    return lax.all_to_all(blocks, PAIR, split_axis=0, concat_axis=0, tiled=True)


def each_pair(move):
    for pair in range(2):
        pl.when(lax.axis_index("pair") == pair)(functools.partial(move, pair))


def to_blocks_kernel(rows_ref, blocks_ref):
    parts, arrays, _, width = blocks_ref.shape

    def move(pair):
        for array in range(arrays):
            for part in range(parts):
                source = (part + pair * parts // 2) % parts
                columns = slice(source * width, (source + 1) * width)
                blocks_ref[part, array] = rows_ref[array, 0, :, columns]

    each_pair(move)


def to_blocks(rows, parts):
    arrays, _, tokens, features = rows.shape
    return pl.pallas_call(
        to_blocks_kernel,
        out_shape=jax.ShapeDtypeStruct((parts, arrays, tokens, features // parts), rows.dtype),
        in_specs=[VMEM],
        out_specs=VMEM,
        compiler_params=PARAMS,
        cost_estimate=pl.CostEstimate(flops=0, bytes_accessed=4 * rows.size, transcendentals=0),
    )(rows)


def to_rows_kernel(blocks_ref, rows_ref):
    parts, _, width = blocks_ref.shape

    def move(pair):
        for part in range(parts):
            target = (part + pair * parts // 2) % parts
            rows_ref[0, :, target * width : (target + 1) * width] = blocks_ref[part]

    each_pair(move)


def to_rows(blocks):
    parts, tokens, width = blocks.shape
    return pl.pallas_call(
        to_rows_kernel,
        out_shape=jax.ShapeDtypeStruct((1, tokens, parts * width), blocks.dtype),
        in_specs=[VMEM],
        out_specs=VMEM,
        compiler_params=PARAMS,
        cost_estimate=pl.CostEstimate(flops=0, bytes_accessed=4 * blocks.size, transcendentals=0),
    )(blocks)


def columns_of(pieces, head):
    rows = pieces[:, :, head * HEAD_DIM : (head + 1) * HEAD_DIM]
    return rows.reshape(rows.shape[0] * rows.shape[1], HEAD_DIM)


def key_of(place, head):
    ref, tile = place
    return columns_of(ref.at[tile, :, 0], head)


def value_of(place, head):
    ref, tile = place
    return columns_of(ref.at[tile, :, 1], head)


def lanes(op, score):
    return functools.reduce(
        op, [score[:, k : k + HEAD_DIM] for k in range(0, score.shape[1], HEAD_DIM)]
    )


def score(query, key):
    return lax.dot_general(query, key, (((1,), (1,)), ((), ())), preferred_element_type=jnp.float32)


def attend(q_ref, out_ref, tile, places):
    _, pieces, piece, width = out_ref.shape
    heads = range(width // HEAD_DIM)
    queries = [columns_of(q_ref.at[tile], head) for head in heads]
    ready = [score(queries[0], key_of(place, 0)) for place in places]
    for head in heads:
        scores, ready = ready, []
        top = functools.reduce(jnp.maximum, [lanes(jnp.maximum, one) for one in scores])
        shift = jnp.max(top, axis=1, keepdims=True) * SCALE
        total, mixed = 0.0, 0.0
        for one, place in zip(scores, places):
            weight = jnp.exp2(one * SCALE - shift)
            total += lanes(jnp.add, weight)
            if head + 1 < len(heads):
                ready.append(score(queries[head + 1], key_of(place, head + 1)))
            mixed += jnp.dot(
                weight.astype(jnp.bfloat16),
                value_of(place, head),
                preferred_element_type=jnp.float32,
            )
        mixed = mixed / jnp.sum(total, axis=1, keepdims=True)
        columns = slice(head * HEAD_DIM, (head + 1) * HEAD_DIM)
        out_ref[tile, :, :, columns] = mixed.astype(jnp.bfloat16).reshape(pieces, piece, HEAD_DIM)


def attend_kernel(pattern_ref, counts_ref, q_ref, own_ref, x_ref, z1_ref, z0_ref, out_ref):
    tiles = out_ref.shape[0]
    last = counts_ref.shape[0] - 1
    slab, pair = lax.axis_index("slab"), lax.axis_index("pair")
    core = lax.rem(lax.axis_index("head"), 2)
    here = counts_ref[slab]
    below = jnp.where(slab >= 1, counts_ref[jnp.maximum(slab - 1, 0)], 0)
    above = jnp.where(slab < last, counts_ref[jnp.minimum(slab + 1, last)], 0)

    @pl.loop(0, tiles)
    def _(tile):
        slot = tiles * pair + tile
        live = slot < here
        left = pattern_ref[slot, 1] == 1
        right = (pattern_ref[slot, 2] == 1) & (slot + 1 < here)
        down = (pattern_ref[slot, 3] == 1) & (slot < below)
        up = (pattern_ref[slot, 4] == 1) & (slot < above)
        inner, outer = (tile == 0, tile == 1)
        others = [
            ((own_ref, 1 - tile), (inner & right) | (outer & left)),
            ((x_ref, 0), (pair != tile) & ((inner & left) | (outer & right))),
            ((z0_ref, tile), ((core == 0) & down) | ((core == 1) & up)),
            ((z1_ref, tile), ((core == 0) & up) | ((core == 1) & down)),
        ]
        code = sum(jnp.where(allowed, 1 << k, 0) for k, (_, allowed) in enumerate(others))
        for subset in range(1 << len(others)):
            places = [(own_ref, tile)]
            places += [place for k, (place, _) in enumerate(others) if subset >> k & 1]
            pl.when(live & (code == subset))(
                functools.partial(attend, q_ref, out_ref, tile, places)
            )

        @pl.when(jnp.logical_not(live))
        def _():
            out_ref[tile] = jnp.zeros(out_ref.shape[1:], jnp.bfloat16)


def on_device(qkv, pattern, counts):
    pair_len, heads = lax.axis_size("lane"), lax.axis_size("head")
    parts = pair_len * heads
    piece, features = qkv.shape[2], qkv.shape[3]
    width = features // parts
    pair = lax.axis_index("pair")
    own = spread(to_blocks(qkv[1:3], parts))
    own, raw_query = lax.optimization_barrier((own, to_blocks(qkv[:1], parts)))
    own = own.reshape(pair_len, heads, 2, piece, width)
    z0 = passed_along(own, 1)
    z1 = passed_along(own, -1)
    x = swapped_across(lax.dynamic_slice_in_dim(own, 1 - pair, 1, axis=0))
    query = spread(raw_query).reshape(pair_len, heads, piece, width)
    attended = pl.pallas_call(
        attend_kernel,
        out_shape=jax.ShapeDtypeStruct(query.shape, jnp.bfloat16),
        in_specs=[SMEM] * 2 + [VMEM] * 5,
        out_specs=VMEM,
        compiler_params=PARAMS,
        cost_estimate=pl.CostEstimate(flops=10**9, bytes_accessed=2**22, transcendentals=0),
    )(pattern, counts, query, own, x, z1, z0)
    return to_rows(spread(attended.reshape(parts, piece, width)))


def solution(mesh):
    slabs, heads, slots = (mesh.shape[axis] for axis in ("slab", "head", "seq"))
    halves = Mesh(mesh.devices.reshape(slabs, heads, 2, slots // 2), ("slab", "head", "pair", "lane"))
    in_specs = (P(None, ("slab", "pair", "lane"), "head", None), P("slab", None), P())
    out_specs = P(("slab", "pair", "lane"), "head", None)
    return jax.shard_map(
        on_device, mesh=halves, in_specs=in_specs, out_specs=out_specs, check_vma=False
    )
```

time: 66 us -> 62.5 us (0.947)
  blocking collectives: 11.5 us -> 24.7 us
  starting transfers between devices: 25.2 us -> 17.5 us
  waiting for transfers between devices: 17.6 us -> 13 us
  Pallas kernels: 8.72 us -> 4.82 us
    all_to_all x1 -> x2, blocking collectives: 11.5 us -> 24.7 us  [spread(): return lax.all_to_all(blocks, PAIR, split_axis=0, concat_axis=0, tiled=True)]
    all_to_all x2 -> x1, waiting for transfers between devices: 17.6 us -> 12 us  [spread(): return lax.all_to_all(blocks, PAIR, split_axis=0, concat_axis=0, tiled=True)]
    ppermute x4 -> x3, starting transfers between devices: 11.5 us -> 7.24 us  [the longest x2 5.32 us: passed_along(): return lax.ppermute(value, ('slab', 'head'), moves)]
    all_to_all x2 -> x1, starting transfers between devices: 13.7 us -> 10.3 us  [spread(): return lax.all_to_all(blocks, PAIR, split_axis=0, concat_axis=0, tiled=True)]
    pallas_call x1, Pallas kernels: 6.24 us -> 3.04 us  [on_device(): pl.pallas_call(attend_kernel, out_shape=jax.ShapeDtypeStruct(query.shape,...]
    ppermute x4 -> x3, waiting for transfers between devices: 0.01 us -> 1.04 us  [the longest x2 1.04 us: passed_along(): return lax.ppermute(value, ('slab', 'head'), moves)]
    pallas_call x2, Pallas kernels: 1.71 us -> 1 us  [to_blocks(): pl.pallas_call(to_blocks_kernel, out_shape=jax.ShapeDtypeStruct((parts, a...]
  transfers between devices with their start and end apart: 6 -> 4, of which waited for: 2 -> 3; matrix products, arithmetic and copies ran while one was open for 2% -> 2% of each run, Pallas kernels for 1% -> 0%
where the time goes in v3:
time: 62.5 us; the launch traced here: 62.4 us
  blocking collectives  24.7 us (40%)
  starting transfers between devices  17.5 us (28%)
  waiting for transfers between devices  13 us (21%)
  Pallas kernels  4.82 us (8%)
  local copies, waits for them, and re-layouts  2.25 us (4%)
    all_to_all x2, blocking collectives, spread(): return lax.all_to_all(blocks, PAIR, split_axis=0, concat_axis=0, tiled=True)  24.7 us
    all_to_all x1, waiting for transfers between devices, spread(): return lax.all_to_all(blocks, PAIR, split_axis=0, concat_axis=0, tiled=True)  12 us
    all_to_all x1, starting transfers between devices, spread(): return lax.all_to_all(blocks, PAIR, split_axis=0, concat_axis=0, tiled=True)  10.3 us
    ppermute x2, starting transfers between devices, passed_along(): return lax.ppermute(value, ('slab', 'head'), moves)  5.32 us
    pallas_call x1, Pallas kernels, on_device(): pl.pallas_call(attend_kernel, out_shape=jax.ShapeDtypeStruct(query.shape,...  3.04 us
    ppermute x1, starting transfers between devices, swapped_across(): lax.ppermute(value, ('pair', 'lane'), [(0, 3), (3, 0), (1, 2), (2, 1)])  1.92 us
  transfers between devices with their start and end apart: 4, of which 3 were waited for; matrix products, arithmetic and copies ran while one was open for 2% of the time, Pallas kernels for 0%

profile of v3, /device:TPU:1, one launch (start us, length us, event | category | flops | bytes accessed | tf_op | source)
XLA Modules:
  0.0 62.4 jit_solution(15633448232429547040)
XLA Ops:
  0.0 1.2 %slice.6.rows_ref = bf16[2,1,48,4096]{3,2,1,0:T(8,128)(2,1)S(1)} slice(bf16[3,1,48,4096]{3,2,1,0:T(8,128)(2,1)} %param.3), slice={[1:3], [0:1], [0:48], [0:4096]} | slice | bytes 1572864 | tf_op jit(solution)/shard_map/slice | solution.py:185
  1.2 1.0 %shard_map.37 = bf16[16,2,48,256]{3,2,1,0:T(8,128)(2,1)} custom-call(bf16[2,1,48,4096]{3,2,1,0:T(8,128)(2,1)S(1)} %slice.6.rows_ref), custom_call_target="tpu_custom_call" | custom-call | bytes 1572864 | tf_op jit(solution)/shard_map/pallas_call | solution.py:59
  2.1 10.3 %all-to-all-start = ((bf16[16,2,48,256]{3,2,1,0:T(8,128)(2,1)}), bf16[16,2,48,256]{3,2,1,0:T(8,128)(2,1)S(1)}, u32[]{:S(2)}, u32[]{:S(2)}) async-start(bf16[16,2,48,256]{3,2,1,0:T(8,128)(2,1)} %shard_map.37), calls=%async_computation | async-start | bytes 1572864 | tf_op jit(solution)/shard_map/all_to_all | solution.py:36
  12.4 1.0 %slice.7.rows_ref = bf16[1,1,48,4096]{3,2,1,0:T(8,128)(2,1)S(1)} slice(bf16[3,1,48,4096]{3,2,1,0:T(8,128)(2,1)} %param.3), slice={[0:1], [0:1], [0:48], [0:4096]} | slice | bytes 786432 | tf_op jit(solution)/shard_map/slice | solution.py:186
  13.5 0.0 copy-start
  13.5 0.0 copy-start.1
  13.5 12.0 %all-to-all-done = bf16[16,2,48,256]{3,2,1,0:T(8,128)(2,1)S(1)} async-done(((bf16[16,2,48,256]{3,2,1,0:T(8,128)(2,1)}), bf16[16,2,48,256]{3,2,1,0:T(8,128)(2,1)S(1)}, u32[]{:S(2)}, u32[]{:S(2)}) %all-to-all-start) | async-done | bytes 786464 | tf_op jit(solution)/shard_map/all_to_all | solution.py:36
  25.5 1.3 %collective-permute-start.2 = (bf16[2,8,2,48,256]{4,3,2,1,0:T(8,128)(2,1)S(1)}, bf16[2,8,2,48,256]{4,3,2,1,0:T(8,128)(2,1)S(1)}, u32[]{:S(2)}, u32[]{:S(2)}) collective-permute-start(bf16[2,8,2,48,256]{4,3,2,1,0:T(8,128)(2,1)S(1)} %bitcast.3), channel_id=1, source_target_pairs={{0,32},{8,40},{16,48},{24,56},{32,64},{36,4},{40,72},{44,12},{48,8... | collective-permute-start | bytes 2359304 | tf_op jit(solution)/shard_map/ppermute | solution.py:28
  26.8 4.0 %collective-permute-start.1 = (bf16[2,8,2,48,256]{4,3,2,1,0:T(8,128)(2,1)S(1)}, bf16[2,8,2,48,256]{4,3,2,1,0:T(8,128)(2,1)S(1)}, u32[]{:S(2)}, u32[]{:S(2)}) collective-permute-start(bf16[2,8,2,48,256]{4,3,2,1,0:T(8,128)(2,1)S(1)} %bitcast.4), channel_id=1, source_target_pairs={{4,36},{12,44},{20,52},{28,60},{32,0},{36,68},{40,8},{44,76},{48,1... | collective-permute-start | bytes 2359304 | tf_op jit(solution)/shard_map/ppermute | solution.py:28
  30.9 1.9 %collective-permute-start = (bf16[1,8,2,48,256]{4,3,2,1,0:T(8,128)(2,1)S(1)}, bf16[1,8,2,48,256]{4,3,2,1,0:T(8,128)(2,1)S(1)}, u32[]{:S(2)}, u32[]{:S(2)}) collective-permute-start(bf16[1,8,2,48,256]{4,3,2,1,0:T(8,128)(2,1)S(1)} %constant_dynamic-slice_fusion), channel_id=1, source_target_pairs={{0,3},{3,0},{1,2},{2,1},{4,7},{7,4},{5,6},{6,5},{8,11},{11,8},{9,1... | collective-permute-start | bytes 1179656 | tf_op jit(solution)/shard_map/ppermute | solution.py:32
  32.8 11.3 %all_to_all.15 = bf16[16,1,48,256]{3,2,1,0:T(8,128)(2,1)S(1)} all-to-all(bf16[16,1,48,256]{3,2,1,0:T(8,128)(2,1)S(1)} %shard_map.38), channel_id=1, replica_groups=mesh['slab'=16,'head'=8,'pair'=2,'lane'=2] {'lane','head'}, dimensions={0} | all-to-all | bytes 786432 | tf_op jit(solution)/shard_map/all_to_all | solution.py:36
  44.1 0.0 collective-permute-done.x_ref
  44.1 0.1 collective-permute-done.2.z0_ref
  44.2 1.0 %collective-permute-done.1.z1_ref = bf16[2,8,2,48,256]{4,3,2,1,0:T(8,128)(2,1)S(1)} collective-permute-done((bf16[2,8,2,48,256]{4,3,2,1,0:T(8,128)(2,1)S(1)}, bf16[2,8,2,48,256]{4,3,2,1,0:T(8,128)(2,1)S(1)}, u32[]{:S(2)}, u32[]{:S(2)}) %collective-permute-start.1) | collective-permute-done | bytes 786464 | tf_op jit(solution)/shard_map/ppermute | solution.py:28
  45.2 0.0 copy-done
  45.2 0.0 copy-done.1
  45.2 3.0 %shard_map.39 = bf16[2,8,48,256]{3,2,1,0:T(8,128)(2,1)S(1)} custom-call(s32[4,5]{1,0:T(4,128)S(1)} %copy-done, s32[16]{0:T(128)S(1)} %copy-done.1, bf16[2,8,48,256]{3,2,1,0:T(8,128)(2,1)S(1)} %bitcast.7, bf16[2,8,2,48,256]{4,3,2,1,0:T(8,128)(2,1)S(1)} %bitcast.6, bf16[1,8,2,48,256]{4,3,2,1,0:T(8,128)(2,1)S(1)} %collective-permute-done.x_ref, ...), custom_call_target="tpu_custom_call" | custom-call | flops 1000000000 | bytes 4194304 | tf_op jit(solution)/shard_map/pallas_call | solution.py:192
  48.2 13.4 %all_to_all.16.blocks_ref = bf16[16,48,256]{2,1,0:T(8,128)(2,1)S(1)} all-to-all(bf16[16,48,256]{2,1,0:T(8,128)(2,1)S(1)} %bitcast.8), channel_id=1, replica_groups=mesh['slab'=16,'head'=8,'pair'=2,'lane'=2] {'lane','head'}, dimensions={0} | all-to-all | bytes 786432 | tf_op jit(solution)/shard_map/all_to_all | solution.py:36
  61.6 0.8 %shard_map.40 = bf16[1,48,4096]{2,1,0:T(8,128)(2,1)} custom-call(bf16[16,48,256]{2,1,0:T(8,128)(2,1)S(1)} %all_to_all.16.blocks_ref), custom_call_target="tpu_custom_call" | custom-call | bytes 786432 | tf_op jit(solution)/shard_map/pallas_call | solution.py:82
  (2 shorter events, 0.1 us)
Async XLA Ops:
  2.1 23.3 %all-to-all-start = ((bf16[16,2,48,256]{3,2,1,0:T(8,128)(2,1)}), bf16[16,2,48,256]{3,2,1,0:T(8,128)(2,1)S(1)}, u32[]{:S(2)}, u32[]{:S(2)}) async-start(bf16[16,2,48,256]{3,2,1,0:T(8,128)(2,1)} %shard_map.37), calls=%async_computation | async-start | bytes 1572864 | tf_op jit(solution)/shard_map/all_to_all | solution.py:36
  13.5 31.7 %copy-start = (s32[4,5]{1,0:T(4,128)S(1)}, s32[4,5]{1,0:T(4,128)}, u32[]{:S(2)}) copy-start(s32[4,5]{1,0:T(4,128)} %pattern_ref.1) | copy-start | bytes 244
  13.5 31.7 %copy-start.1 = (s32[16]{0:T(128)S(1)}, s32[16]{0:T(128)}, u32[]{:S(2)}) copy-start(s32[16]{0:T(128)} %counts_ref.1) | copy-start | bytes 196
  25.5 18.7 %collective-permute-start.2 = (bf16[2,8,2,48,256]{4,3,2,1,0:T(8,128)(2,1)S(1)}, bf16[2,8,2,48,256]{4,3,2,1,0:T(8,128)(2,1)S(1)}, u32[]{:S(2)}, u32[]{:S(2)}) collective-permute-start(bf16[2,8,2,48,256]{4,3,2,1,0:T(8,128)(2,1)S(1)} %bitcast.3), channel_id=1, source_target_pairs={{0,32},{8,40},{16,48},{24,56},{32,64},{36,4},{40,72},{44,12},{48,8... | collective-permute-start | bytes 2359304 | tf_op jit(solution)/shard_map/ppermute | solution.py:28
  26.8 18.4 %collective-permute-start.1 = (bf16[2,8,2,48,256]{4,3,2,1,0:T(8,128)(2,1)S(1)}, bf16[2,8,2,48,256]{4,3,2,1,0:T(8,128)(2,1)S(1)}, u32[]{:S(2)}, u32[]{:S(2)}) collective-permute-start(bf16[2,8,2,48,256]{4,3,2,1,0:T(8,128)(2,1)S(1)} %bitcast.4), channel_id=1, source_target_pairs={{4,36},{12,44},{20,52},{28,60},{32,0},{36,68},{40,8},{44,76},{48,1... | collective-permute-start | bytes 2359304 | tf_op jit(solution)/shard_map/ppermute | solution.py:28
  30.9 13.3 %collective-permute-start = (bf16[1,8,2,48,256]{4,3,2,1,0:T(8,128)(2,1)S(1)}, bf16[1,8,2,48,256]{4,3,2,1,0:T(8,128)(2,1)S(1)}, u32[]{:S(2)}, u32[]{:S(2)}) collective-permute-start(bf16[1,8,2,48,256]{4,3,2,1,0:T(8,128)(2,1)S(1)} %constant_dynamic-slice_fusion), channel_id=1, source_target_pairs={{0,3},{3,0},{1,2},{2,1},{4,7},{7,4},{5,6},{6,5},{8,11},{11,8},{9,1... | collective-permute-start | bytes 1179656 | tf_op jit(solution)/shard_map/ppermute | solution.py:32

commit v4 on v3

--- a/solution.py
+++ b/solution.py
@@ -163,13 +163,15 @@
             ((z0_ref, tile), ((core == 0) & down) | ((core == 1) & up)),
             ((z1_ref, tile), ((core == 0) & up) | ((core == 1) & down)),
         ]
-        code = sum(jnp.where(allowed, 1 << k, 0) for k, (_, allowed) in enumerate(others))
-        for subset in range(1 << len(others)):
-            places = [(own_ref, tile)]
-            places += [place for k, (place, _) in enumerate(others) if subset >> k & 1]
-            pl.when(live & (code == subset))(
-                functools.partial(attend, q_ref, out_ref, tile, places)
-            )
+        def choose(k, places):
+            if k == len(others):
+                attend(q_ref, out_ref, tile, places)
+                return
+            place, allowed = others[k]
+            pl.when(allowed)(lambda: choose(k + 1, places + [place]))
+            pl.when(jnp.logical_not(allowed))(lambda: choose(k + 1, places))
+
+        pl.when(live)(lambda: choose(0, [(own_ref, tile)]))
 
         @pl.when(jnp.logical_not(live))
         def _():

time: 62.5 us -> 62.2 us (level); the launches traced: 62.4 us -> 61.1 us
  Pallas kernels: 4.82 us -> 3.56 us
    pallas_call x1, Pallas kernels: 3.04 us -> 1.79 us  [on_device(): pl.pallas_call(attend_kernel, out_shape=jax.ShapeDtypeStruct(query.shape,...]
where the time goes in v4:
time: 62.2 us; the launch traced here: 61.1 us
  blocking collectives  24.7 us (40%)
  starting transfers between devices  17.5 us (28%)
  waiting for transfers between devices  13 us (21%)
  Pallas kernels  3.56 us (6%)
  local copies, waits for them, and re-layouts  2.25 us (4%)
    all_to_all x2, blocking collectives, spread(): return lax.all_to_all(blocks, PAIR, split_axis=0, concat_axis=0, tiled=True)  24.7 us
    all_to_all x1, waiting for transfers between devices, spread(): return lax.all_to_all(blocks, PAIR, split_axis=0, concat_axis=0, tiled=True)  12 us
    all_to_all x1, starting transfers between devices, spread(): return lax.all_to_all(blocks, PAIR, split_axis=0, concat_axis=0, tiled=True)  10.3 us
    ppermute x2, starting transfers between devices, passed_along(): return lax.ppermute(value, ('slab', 'head'), moves)  5.32 us
    ppermute x1, starting transfers between devices, swapped_across(): lax.ppermute(value, ('pair', 'lane'), [(0, 3), (3, 0), (1, 2), (2, 1)])  1.92 us
    pallas_call x1, Pallas kernels, on_device(): pl.pallas_call(attend_kernel, out_shape=jax.ShapeDtypeStruct(query.shape,...  1.79 us
  transfers between devices with their start and end apart: 4, of which 3 were waited for; matrix products, arithmetic and copies ran while one was open for 2% of the time, Pallas kernels for 0%

profile of v4, /device:TPU:1, one launch (start us, length us, event | category | flops | bytes accessed | tf_op | source)
XLA Modules:
  0.0 61.1 jit_solution(17879650959984300493)
XLA Ops:
  0.0 1.2 %slice.6.rows_ref = bf16[2,1,48,4096]{3,2,1,0:T(8,128)(2,1)S(1)} slice(bf16[3,1,48,4096]{3,2,1,0:T(8,128)(2,1)} %param.3), slice={[1:3], [0:1], [0:48], [0:4096]} | slice | bytes 1572864 | tf_op jit(solution)/shard_map/slice | solution.py:187
  1.2 1.0 %shard_map.37 = bf16[16,2,48,256]{3,2,1,0:T(8,128)(2,1)} custom-call(bf16[2,1,48,4096]{3,2,1,0:T(8,128)(2,1)S(1)} %slice.6.rows_ref), custom_call_target="tpu_custom_call" | custom-call | bytes 1572864 | tf_op jit(solution)/shard_map/pallas_call | solution.py:59
  2.1 10.3 %all-to-all-start = ((bf16[16,2,48,256]{3,2,1,0:T(8,128)(2,1)}), bf16[16,2,48,256]{3,2,1,0:T(8,128)(2,1)S(1)}, u32[]{:S(2)}, u32[]{:S(2)}) async-start(bf16[16,2,48,256]{3,2,1,0:T(8,128)(2,1)} %shard_map.37), calls=%async_computation | async-start | bytes 1572864 | tf_op jit(solution)/shard_map/all_to_all | solution.py:36
  12.4 1.0 %slice.7.rows_ref = bf16[1,1,48,4096]{3,2,1,0:T(8,128)(2,1)S(1)} slice(bf16[3,1,48,4096]{3,2,1,0:T(8,128)(2,1)} %param.3), slice={[0:1], [0:1], [0:48], [0:4096]} | slice | bytes 786432 | tf_op jit(solution)/shard_map/slice | solution.py:188
  13.5 0.0 copy-start
  13.5 0.0 copy-start.1
  13.5 12.0 %all-to-all-done = bf16[16,2,48,256]{3,2,1,0:T(8,128)(2,1)S(1)} async-done(((bf16[16,2,48,256]{3,2,1,0:T(8,128)(2,1)}), bf16[16,2,48,256]{3,2,1,0:T(8,128)(2,1)S(1)}, u32[]{:S(2)}, u32[]{:S(2)}) %all-to-all-start) | async-done | bytes 786464 | tf_op jit(solution)/shard_map/all_to_all | solution.py:36
  25.5 1.3 %collective-permute-start.2 = (bf16[2,8,2,48,256]{4,3,2,1,0:T(8,128)(2,1)S(1)}, bf16[2,8,2,48,256]{4,3,2,1,0:T(8,128)(2,1)S(1)}, u32[]{:S(2)}, u32[]{:S(2)}) collective-permute-start(bf16[2,8,2,48,256]{4,3,2,1,0:T(8,128)(2,1)S(1)} %bitcast.3), channel_id=1, source_target_pairs={{0,32},{8,40},{16,48},{24,56},{32,64},{36,4},{40,72},{44,12},{48,8... | collective-permute-start | bytes 2359304 | tf_op jit(solution)/shard_map/ppermute | solution.py:28
  26.8 4.0 %collective-permute-start.1 = (bf16[2,8,2,48,256]{4,3,2,1,0:T(8,128)(2,1)S(1)}, bf16[2,8,2,48,256]{4,3,2,1,0:T(8,128)(2,1)S(1)}, u32[]{:S(2)}, u32[]{:S(2)}) collective-permute-start(bf16[2,8,2,48,256]{4,3,2,1,0:T(8,128)(2,1)S(1)} %bitcast.4), channel_id=1, source_target_pairs={{4,36},{12,44},{20,52},{28,60},{32,0},{36,68},{40,8},{44,76},{48,1... | collective-permute-start | bytes 2359304 | tf_op jit(solution)/shard_map/ppermute | solution.py:28
  30.9 1.9 %collective-permute-start = (bf16[1,8,2,48,256]{4,3,2,1,0:T(8,128)(2,1)S(1)}, bf16[1,8,2,48,256]{4,3,2,1,0:T(8,128)(2,1)S(1)}, u32[]{:S(2)}, u32[]{:S(2)}) collective-permute-start(bf16[1,8,2,48,256]{4,3,2,1,0:T(8,128)(2,1)S(1)} %constant_dynamic-slice_fusion), channel_id=1, source_target_pairs={{0,3},{3,0},{1,2},{2,1},{4,7},{7,4},{5,6},{6,5},{8,11},{11,8},{9,1... | collective-permute-start | bytes 1179656 | tf_op jit(solution)/shard_map/ppermute | solution.py:32
  32.8 11.3 %all_to_all.15 = bf16[16,1,48,256]{3,2,1,0:T(8,128)(2,1)S(1)} all-to-all(bf16[16,1,48,256]{3,2,1,0:T(8,128)(2,1)S(1)} %shard_map.38), channel_id=1, replica_groups=mesh['slab'=16,'head'=8,'pair'=2,'lane'=2] {'lane','head'}, dimensions={0} | all-to-all | bytes 786432 | tf_op jit(solution)/shard_map/all_to_all | solution.py:36
  44.1 0.0 collective-permute-done.x_ref
  44.1 0.1 collective-permute-done.2.z0_ref
  44.2 1.0 %collective-permute-done.1.z1_ref = bf16[2,8,2,48,256]{4,3,2,1,0:T(8,128)(2,1)S(1)} collective-permute-done((bf16[2,8,2,48,256]{4,3,2,1,0:T(8,128)(2,1)S(1)}, bf16[2,8,2,48,256]{4,3,2,1,0:T(8,128)(2,1)S(1)}, u32[]{:S(2)}, u32[]{:S(2)}) %collective-permute-start.1) | collective-permute-done | bytes 786464 | tf_op jit(solution)/shard_map/ppermute | solution.py:28
  45.2 0.0 copy-done
  45.2 0.0 copy-done.1
  45.2 1.8 %shard_map.39 = bf16[2,8,48,256]{3,2,1,0:T(8,128)(2,1)S(1)} custom-call(s32[4,5]{1,0:T(4,128)S(1)} %copy-done, s32[16]{0:T(128)S(1)} %copy-done.1, bf16[2,8,48,256]{3,2,1,0:T(8,128)(2,1)S(1)} %bitcast.7, bf16[2,8,2,48,256]{4,3,2,1,0:T(8,128)(2,1)S(1)} %bitcast.6, bf16[1,8,2,48,256]{4,3,2,1,0:T(8,128)(2,1)S(1)} %collective-permute-done.x_ref, ...), custom_call_target="tpu_custom_call" | custom-call | flops 1000000000 | bytes 4194304 | tf_op jit(solution)/shard_map/pallas_call | solution.py:194
  47.0 13.4 %all_to_all.16.blocks_ref = bf16[16,48,256]{2,1,0:T(8,128)(2,1)S(1)} all-to-all(bf16[16,48,256]{2,1,0:T(8,128)(2,1)S(1)} %bitcast.8), channel_id=1, replica_groups=mesh['slab'=16,'head'=8,'pair'=2,'lane'=2] {'lane','head'}, dimensions={0} | all-to-all | bytes 786432 | tf_op jit(solution)/shard_map/all_to_all | solution.py:36
  60.4 0.8 %shard_map.40 = bf16[1,48,4096]{2,1,0:T(8,128)(2,1)} custom-call(bf16[16,48,256]{2,1,0:T(8,128)(2,1)S(1)} %all_to_all.16.blocks_ref), custom_call_target="tpu_custom_call" | custom-call | bytes 786432 | tf_op jit(solution)/shard_map/pallas_call | solution.py:82
  (2 shorter events, 0.1 us)
Async XLA Ops:
  2.1 23.3 %all-to-all-start = ((bf16[16,2,48,256]{3,2,1,0:T(8,128)(2,1)}), bf16[16,2,48,256]{3,2,1,0:T(8,128)(2,1)S(1)}, u32[]{:S(2)}, u32[]{:S(2)}) async-start(bf16[16,2,48,256]{3,2,1,0:T(8,128)(2,1)} %shard_map.37), calls=%async_computation | async-start | bytes 1572864 | tf_op jit(solution)/shard_map/all_to_all | solution.py:36
  13.5 31.7 %copy-start = (s32[4,5]{1,0:T(4,128)S(1)}, s32[4,5]{1,0:T(4,128)}, u32[]{:S(2)}) copy-start(s32[4,5]{1,0:T(4,128)} %pattern_ref.1) | copy-start | bytes 244
  13.5 31.7 %copy-start.1 = (s32[16]{0:T(128)S(1)}, s32[16]{0:T(128)}, u32[]{:S(2)}) copy-start(s32[16]{0:T(128)} %counts_ref.1) | copy-start | bytes 196
  25.5 18.7 %collective-permute-start.2 = (bf16[2,8,2,48,256]{4,3,2,1,0:T(8,128)(2,1)S(1)}, bf16[2,8,2,48,256]{4,3,2,1,0:T(8,128)(2,1)S(1)}, u32[]{:S(2)}, u32[]{:S(2)}) collective-permute-start(bf16[2,8,2,48,256]{4,3,2,1,0:T(8,128)(2,1)S(1)} %bitcast.3), channel_id=1, source_target_pairs={{0,32},{8,40},{16,48},{24,56},{32,64},{36,4},{40,72},{44,12},{48,8... | collective-permute-start | bytes 2359304 | tf_op jit(solution)/shard_map/ppermute | solution.py:28
  26.8 18.4 %collective-permute-start.1 = (bf16[2,8,2,48,256]{4,3,2,1,0:T(8,128)(2,1)S(1)}, bf16[2,8,2,48,256]{4,3,2,1,0:T(8,128)(2,1)S(1)}, u32[]{:S(2)}, u32[]{:S(2)}) collective-permute-start(bf16[2,8,2,48,256]{4,3,2,1,0:T(8,128)(2,1)S(1)} %bitcast.4), channel_id=1, source_target_pairs={{4,36},{12,44},{20,52},{28,60},{32,0},{36,68},{40,8},{44,76},{48,1... | collective-permute-start | bytes 2359304 | tf_op jit(solution)/shard_map/ppermute | solution.py:28
  30.9 13.3 %collective-permute-start = (bf16[1,8,2,48,256]{4,3,2,1,0:T(8,128)(2,1)S(1)}, bf16[1,8,2,48,256]{4,3,2,1,0:T(8,128)(2,1)S(1)}, u32[]{:S(2)}, u32[]{:S(2)}) collective-permute-start(bf16[1,8,2,48,256]{4,3,2,1,0:T(8,128)(2,1)S(1)} %constant_dynamic-slice_fusion), channel_id=1, source_target_pairs={{0,3},{3,0},{1,2},{2,1},{4,7},{7,4},{5,6},{6,5},{8,11},{11,8},{9,1... | collective-permute-start | bytes 1179656 | tf_op jit(solution)/shard_map/ppermute | solution.py:32

commit v5 on v4

--- a/solution.py
+++ b/solution.py
@@ -10,6 +10,8 @@
 from jax.sharding import PartitionSpec as P
 
 HEAD_DIM = 128
+LARGE = 1e30
+BLOCKED = -1e30
 PAIR = ("lane", "head")
 SCALE = math.log2(math.e) / math.sqrt(HEAD_DIM)
 SMEM = pl.BlockSpec(memory_space=pltpu.SMEM)
@@ -114,15 +116,15 @@
     return lax.dot_general(query, key, (((1,), (1,)), ((), ())), preferred_element_type=jnp.float32)
 
 
-def attend(q_ref, out_ref, tile, places):
+def attend(q_ref, out_ref, flag_ref, tile, places):
     _, pieces, piece, width = out_ref.shape
     heads = range(width // HEAD_DIM)
     queries = [columns_of(q_ref.at[tile], head) for head in heads]
     ready = [score(queries[0], key_of(place, 0)) for place in places]
+    largest = 0.0
     for head in heads:
         scores, ready = ready, []
-        top = functools.reduce(jnp.maximum, [lanes(jnp.maximum, one) for one in scores])
-        shift = jnp.max(top, axis=1, keepdims=True) * SCALE
+        shift = jnp.max(lanes(jnp.maximum, scores[0]), axis=1, keepdims=True) * SCALE
         total, mixed = 0.0, 0.0
         for one, place in zip(scores, places):
             weight = jnp.exp2(one * SCALE - shift)
@@ -134,12 +136,39 @@
                 value_of(place, head),
                 preferred_element_type=jnp.float32,
             )
+        largest = jnp.maximum(largest, total)
         mixed = mixed / jnp.sum(total, axis=1, keepdims=True)
         columns = slice(head * HEAD_DIM, (head + 1) * HEAD_DIM)
         out_ref[tile, :, :, columns] = mixed.astype(jnp.bfloat16).reshape(pieces, piece, HEAD_DIM)
-
-
-def attend_kernel(pattern_ref, counts_ref, q_ref, own_ref, x_ref, z1_ref, z0_ref, out_ref):
+    if len(places) > 1:
+        flag_ref[0] = jnp.where(jnp.max(largest) < LARGE, 0, 1)
+
+
+def attend_safely(q_ref, out_ref, tile, asked):
+    _, pieces, piece, width = out_ref.shape
+    for head in range(width // HEAD_DIM):
+        query = columns_of(q_ref.at[tile], head)
+        scores = [score(query, key_of(place, head)) for place, _ in asked]
+        biases = [jnp.where(allowed, 0.0, BLOCKED) for _, allowed in asked]
+        tops = [lanes(jnp.maximum, one) + bias for one, bias in zip(scores, biases)]
+        peak = jnp.max(functools.reduce(jnp.maximum, tops), axis=1, keepdims=True)
+        total, mixed = 0.0, 0.0
+        for one, bias, (place, _) in zip(scores, biases, asked):
+            weight = jnp.exp2(one * SCALE + (bias - peak) * SCALE)
+            total += lanes(jnp.add, weight)
+            mixed += jnp.dot(
+                weight.astype(jnp.bfloat16),
+                value_of(place, head),
+                preferred_element_type=jnp.float32,
+            )
+        mixed = mixed / jnp.sum(total, axis=1, keepdims=True)
+        columns = slice(head * HEAD_DIM, (head + 1) * HEAD_DIM)
+        out_ref[tile, :, :, columns] = mixed.astype(jnp.bfloat16).reshape(pieces, piece, HEAD_DIM)
+
+
+def attend_kernel(
+    pattern_ref, counts_ref, q_ref, own_ref, x_ref, z1_ref, z0_ref, out_ref, flag_ref
+):
     tiles = out_ref.shape[0]
     last = counts_ref.shape[0] - 1
     slab, pair = lax.axis_index("slab"), lax.axis_index("pair")
@@ -163,15 +192,20 @@
             ((z0_ref, tile), ((core == 0) & down) | ((core == 1) & up)),
             ((z1_ref, tile), ((core == 0) & up) | ((core == 1) & down)),
         ]
+        flag_ref[0] = 0
         def choose(k, places):
             if k == len(others):
-                attend(q_ref, out_ref, tile, places)
+                attend(q_ref, out_ref, flag_ref, tile, places)
                 return
             place, allowed = others[k]
             pl.when(allowed)(lambda: choose(k + 1, places + [place]))
             pl.when(jnp.logical_not(allowed))(lambda: choose(k + 1, places))
 
         pl.when(live)(lambda: choose(0, [(own_ref, tile)]))
+
+        asked = [((own_ref, tile), True)] + others
+        unsafe = live & (flag_ref[0] == 1)
+        pl.when(unsafe)(functools.partial(attend_safely, q_ref, out_ref, tile, asked))
 
         @pl.when(jnp.logical_not(live))
         def _():
@@ -196,6 +230,7 @@
         out_shape=jax.ShapeDtypeStruct(query.shape, jnp.bfloat16),
         in_specs=[SMEM] * 2 + [VMEM] * 5,
         out_specs=VMEM,
+        scratch_shapes=[pltpu.SMEM((1,), jnp.int32)],
         compiler_params=PARAMS,
         cost_estimate=pl.CostEstimate(flops=10**9, bytes_accessed=2**22, transcendentals=0),
     )(pattern, counts, query, own, x, z1, z0)

time: 62.2 us -> 61.7 us (level)
  no operation moved by 1% of the time
where the time goes in v5:
time: 61.7 us; the launch traced here: 61.1 us
  blocking collectives  24.7 us (40%)
  starting transfers between devices  17.5 us (28%)
  waiting for transfers between devices  13 us (21%)
  Pallas kernels  3.48 us (6%)
  local copies, waits for them, and re-layouts  2.25 us (4%)
    all_to_all x2, blocking collectives, spread(): return lax.all_to_all(blocks, PAIR, split_axis=0, concat_axis=0, tiled=True)  24.7 us
    all_to_all x1, waiting for transfers between devices, spread(): return lax.all_to_all(blocks, PAIR, split_axis=0, concat_axis=0, tiled=True)  12 us
    all_to_all x1, starting transfers between devices, spread(): return lax.all_to_all(blocks, PAIR, split_axis=0, concat_axis=0, tiled=True)  10.3 us
    ppermute x2, starting transfers between devices, passed_along(): return lax.ppermute(value, ('slab', 'head'), moves)  5.32 us
    ppermute x1, starting transfers between devices, swapped_across(): lax.ppermute(value, ('pair', 'lane'), [(0, 3), (3, 0), (1, 2), (2, 1)])  1.92 us
    pallas_call x1, Pallas kernels, on_device(): pl.pallas_call(attend_kernel, out_shape=jax.ShapeDtypeStruct(query.shape,...  1.71 us
  transfers between devices with their start and end apart: 4, of which 3 were waited for; matrix products, arithmetic and copies ran while one was open for 2% of the time, Pallas kernels for 0%

profile of v5, /device:TPU:1, one launch (start us, length us, event | category | flops | bytes accessed | tf_op | source)
XLA Modules:
  0.0 61.1 jit_solution(9041714388795554519)
XLA Ops:
  0.0 1.2 %slice.6.rows_ref = bf16[2,1,48,4096]{3,2,1,0:T(8,128)(2,1)S(1)} slice(bf16[3,1,48,4096]{3,2,1,0:T(8,128)(2,1)} %param.3), slice={[1:3], [0:1], [0:48], [0:4096]} | slice | bytes 1572864 | tf_op jit(solution)/shard_map/slice | solution.py:221
  1.2 1.0 %shard_map.37 = bf16[16,2,48,256]{3,2,1,0:T(8,128)(2,1)} custom-call(bf16[2,1,48,4096]{3,2,1,0:T(8,128)(2,1)S(1)} %slice.6.rows_ref), custom_call_target="tpu_custom_call" | custom-call | bytes 1572864 | tf_op jit(solution)/shard_map/pallas_call | solution.py:61
  2.1 10.3 %all-to-all-start = ((bf16[16,2,48,256]{3,2,1,0:T(8,128)(2,1)}), bf16[16,2,48,256]{3,2,1,0:T(8,128)(2,1)S(1)}, u32[]{:S(2)}, u32[]{:S(2)}) async-start(bf16[16,2,48,256]{3,2,1,0:T(8,128)(2,1)} %shard_map.37), calls=%async_computation | async-start | bytes 1572864 | tf_op jit(solution)/shard_map/all_to_all | solution.py:38
  12.4 1.0 %slice.7.rows_ref = bf16[1,1,48,4096]{3,2,1,0:T(8,128)(2,1)S(1)} slice(bf16[3,1,48,4096]{3,2,1,0:T(8,128)(2,1)} %param.3), slice={[0:1], [0:1], [0:48], [0:4096]} | slice | bytes 786432 | tf_op jit(solution)/shard_map/slice | solution.py:222
  13.5 0.0 copy-start
  13.5 0.0 copy-start.1
  13.5 12.0 %all-to-all-done = bf16[16,2,48,256]{3,2,1,0:T(8,128)(2,1)S(1)} async-done(((bf16[16,2,48,256]{3,2,1,0:T(8,128)(2,1)}), bf16[16,2,48,256]{3,2,1,0:T(8,128)(2,1)S(1)}, u32[]{:S(2)}, u32[]{:S(2)}) %all-to-all-start) | async-done | bytes 786464 | tf_op jit(solution)/shard_map/all_to_all | solution.py:38
  25.5 1.3 %collective-permute-start.2 = (bf16[2,8,2,48,256]{4,3,2,1,0:T(8,128)(2,1)S(1)}, bf16[2,8,2,48,256]{4,3,2,1,0:T(8,128)(2,1)S(1)}, u32[]{:S(2)}, u32[]{:S(2)}) collective-permute-start(bf16[2,8,2,48,256]{4,3,2,1,0:T(8,128)(2,1)S(1)} %bitcast.3), channel_id=1, source_target_pairs={{0,32},{8,40},{16,48},{24,56},{32,64},{36,4},{40,72},{44,12},{48,8... | collective-permute-start | bytes 2359304 | tf_op jit(solution)/shard_map/ppermute | solution.py:30
  26.8 4.0 %collective-permute-start.1 = (bf16[2,8,2,48,256]{4,3,2,1,0:T(8,128)(2,1)S(1)}, bf16[2,8,2,48,256]{4,3,2,1,0:T(8,128)(2,1)S(1)}, u32[]{:S(2)}, u32[]{:S(2)}) collective-permute-start(bf16[2,8,2,48,256]{4,3,2,1,0:T(8,128)(2,1)S(1)} %bitcast.4), channel_id=1, source_target_pairs={{4,36},{12,44},{20,52},{28,60},{32,0},{36,68},{40,8},{44,76},{48,1... | collective-permute-start | bytes 2359304 | tf_op jit(solution)/shard_map/ppermute | solution.py:30
  30.9 1.9 %collective-permute-start = (bf16[1,8,2,48,256]{4,3,2,1,0:T(8,128)(2,1)S(1)}, bf16[1,8,2,48,256]{4,3,2,1,0:T(8,128)(2,1)S(1)}, u32[]{:S(2)}, u32[]{:S(2)}) collective-permute-start(bf16[1,8,2,48,256]{4,3,2,1,0:T(8,128)(2,1)S(1)} %constant_dynamic-slice_fusion), channel_id=1, source_target_pairs={{0,3},{3,0},{1,2},{2,1},{4,7},{7,4},{5,6},{6,5},{8,11},{11,8},{9,1... | collective-permute-start | bytes 1179656 | tf_op jit(solution)/shard_map/ppermute | solution.py:34
  32.8 11.3 %all_to_all.15 = bf16[16,1,48,256]{3,2,1,0:T(8,128)(2,1)S(1)} all-to-all(bf16[16,1,48,256]{3,2,1,0:T(8,128)(2,1)S(1)} %shard_map.38), channel_id=1, replica_groups=mesh['slab'=16,'head'=8,'pair'=2,'lane'=2] {'lane','head'}, dimensions={0} | all-to-all | bytes 786432 | tf_op jit(solution)/shard_map/all_to_all | solution.py:38
  44.1 0.0 collective-permute-done.x_ref
  44.1 0.1 collective-permute-done.2.z0_ref
  44.2 1.0 %collective-permute-done.1.z1_ref = bf16[2,8,2,48,256]{4,3,2,1,0:T(8,128)(2,1)S(1)} collective-permute-done((bf16[2,8,2,48,256]{4,3,2,1,0:T(8,128)(2,1)S(1)}, bf16[2,8,2,48,256]{4,3,2,1,0:T(8,128)(2,1)S(1)}, u32[]{:S(2)}, u32[]{:S(2)}) %collective-permute-start.1) | collective-permute-done | bytes 786464 | tf_op jit(solution)/shard_map/ppermute | solution.py:30
  45.2 0.0 copy-done
  45.2 0.0 copy-done.1
  45.2 1.7 %shard_map.39 = bf16[2,8,48,256]{3,2,1,0:T(8,128)(2,1)S(1)} custom-call(s32[4,5]{1,0:T(4,128)S(1)} %copy-done, s32[16]{0:T(128)S(1)} %copy-done.1, bf16[2,8,48,256]{3,2,1,0:T(8,128)(2,1)S(1)} %bitcast.7, bf16[2,8,2,48,256]{4,3,2,1,0:T(8,128)(2,1)S(1)} %bitcast.6, bf16[1,8,2,48,256]{4,3,2,1,0:T(8,128)(2,1)S(1)} %collective-permute-done.x_ref, ...), custom_call_target="tpu_custom_call" | custom-call | flops 1000000000 | bytes 4194304 | tf_op jit(solution)/shard_map/pallas_call | solution.py:228
  46.9 13.4 %all_to_all.16.blocks_ref = bf16[16,48,256]{2,1,0:T(8,128)(2,1)S(1)} all-to-all(bf16[16,48,256]{2,1,0:T(8,128)(2,1)S(1)} %bitcast.8), channel_id=1, replica_groups=mesh['slab'=16,'head'=8,'pair'=2,'lane'=2] {'lane','head'}, dimensions={0} | all-to-all | bytes 786432 | tf_op jit(solution)/shard_map/all_to_all | solution.py:38
  60.3 0.8 %shard_map.40 = bf16[1,48,4096]{2,1,0:T(8,128)(2,1)} custom-call(bf16[16,48,256]{2,1,0:T(8,128)(2,1)S(1)} %all_to_all.16.blocks_ref), custom_call_target="tpu_custom_call" | custom-call | bytes 786432 | tf_op jit(solution)/shard_map/pallas_call | solution.py:84
  (2 shorter events, 0.1 us)
Async XLA Ops:
  2.1 23.3 %all-to-all-start = ((bf16[16,2,48,256]{3,2,1,0:T(8,128)(2,1)}), bf16[16,2,48,256]{3,2,1,0:T(8,128)(2,1)S(1)}, u32[]{:S(2)}, u32[]{:S(2)}) async-start(bf16[16,2,48,256]{3,2,1,0:T(8,128)(2,1)} %shard_map.37), calls=%async_computation | async-start | bytes 1572864 | tf_op jit(solution)/shard_map/all_to_all | solution.py:38
  13.5 31.7 %copy-start = (s32[4,5]{1,0:T(4,128)S(1)}, s32[4,5]{1,0:T(4,128)}, u32[]{:S(2)}) copy-start(s32[4,5]{1,0:T(4,128)} %pattern_ref.1) | copy-start | bytes 244
  13.5 31.7 %copy-start.1 = (s32[16]{0:T(128)S(1)}, s32[16]{0:T(128)}, u32[]{:S(2)}) copy-start(s32[16]{0:T(128)} %counts_ref.1) | copy-start | bytes 196
  25.5 18.7 %collective-permute-start.2 = (bf16[2,8,2,48,256]{4,3,2,1,0:T(8,128)(2,1)S(1)}, bf16[2,8,2,48,256]{4,3,2,1,0:T(8,128)(2,1)S(1)}, u32[]{:S(2)}, u32[]{:S(2)}) collective-permute-start(bf16[2,8,2,48,256]{4,3,2,1,0:T(8,128)(2,1)S(1)} %bitcast.3), channel_id=1, source_target_pairs={{0,32},{8,40},{16,48},{24,56},{32,64},{36,4},{40,72},{44,12},{48,8... | collective-permute-start | bytes 2359304 | tf_op jit(solution)/shard_map/ppermute | solution.py:30
  26.8 18.4 %collective-permute-start.1 = (bf16[2,8,2,48,256]{4,3,2,1,0:T(8,128)(2,1)S(1)}, bf16[2,8,2,48,256]{4,3,2,1,0:T(8,128)(2,1)S(1)}, u32[]{:S(2)}, u32[]{:S(2)}) collective-permute-start(bf16[2,8,2,48,256]{4,3,2,1,0:T(8,128)(2,1)S(1)} %bitcast.4), channel_id=1, source_target_pairs={{4,36},{12,44},{20,52},{28,60},{32,0},{36,68},{40,8},{44,76},{48,1... | collective-permute-start | bytes 2359304 | tf_op jit(solution)/shard_map/ppermute | solution.py:30
  30.9 13.3 %collective-permute-start = (bf16[1,8,2,48,256]{4,3,2,1,0:T(8,128)(2,1)S(1)}, bf16[1,8,2,48,256]{4,3,2,1,0:T(8,128)(2,1)S(1)}, u32[]{:S(2)}, u32[]{:S(2)}) collective-permute-start(bf16[1,8,2,48,256]{4,3,2,1,0:T(8,128)(2,1)S(1)} %constant_dynamic-slice_fusion), channel_id=1, source_target_pairs={{0,3},{3,0},{1,2},{2,1},{4,7},{7,4},{5,6},{6,5},{8,11},{11,8},{9,1... | collective-permute-start | bytes 1179656 | tf_op jit(solution)/shard_map/ppermute | solution.py:34
